TPU v7x, 512 devices: a whole 4x4x16 slice. The times are simulated.
512 devices in a mesh: feat: 16 (over z), batch: 32 (over y, x, core).
Axes of the slice: x: 4, y: 4, z: 16, core: 2. Of those that a mesh axis runs over, the one named last changes fastest.
Arguments:
- feats: bfloat16 [32, 768, 8192], P('batch', 'feat'), may hold values from -6 to 6
- nbr_one: int32 [32, 15, 1024], P('batch'), may hold values from 0 to 8191
- rel_one: int32 [32, 15, 1024], P('batch'), may hold values from 0 to 4
- w_one: bfloat16 [5, 768, 1024], P(None, 'feat'), may hold values from -0.09375 to 0.09375
- owner_two: int32 [32, 1024, 10, 1], P('batch'), may hold values from 0 to 31; in each aligned block of 640 rows (0 to 639, 640 to 1279, ..., all dimensions but the last counted through in order) at most 40 rows name the same one
- local_two: int32 [32, 1024, 10], P('batch'), may hold values from 0 to 63
- rel_two: int32 [32, 1024, 10], P('batch'), may hold values from 0 to 4
- w_two: bfloat16 [5, 1024, 1024], P(None, 'feat'), may hold values from -0.078125 to 0.078125
Outputs:
- hidden_two: bfloat16 [32, 1024, 1024], P('batch', 'feat')
Inputs may be any that keep to these rules, and one draw needn't show every extreme that they name: `owner_two`: every neighbour of destination j lies in the block of rows (j // 64) * 64 to (j // 64) * 64 + 63 of its mini-batch; among the 640 edges of each aligned block of 64 destinations, no mini-batch is named more than 40 times. `rel_one`: the value 4 marks an empty slot. `rel_two`: the value 4 marks an empty slot.
All inputs are finite; a program needn't handle non-finite values.
Results may differ from a plain program's by a relative error of at most 0.025.
Values may be sent and summed in bfloat16 or wider, within the bound.
A program may use at most 64 MiB of HBM per device.

v0:
```python
import jax
import jax.numpy as jnp
from jax import lax
from jax.sharding import PartitionSpec as P

RELATIONS = 4
FANOUT_TWO = 10
ROWS = 64


def relation_counts(relation_ids, along):
    counted = [
        jnp.maximum(jnp.sum((relation_ids == relation).astype(jnp.int32), axis=along), 1)
        for relation in range(RELATIONS)
    ]
    return jnp.stack(counted).astype(jnp.float32)


def first_means(columns, neighbours, relation_ids):
    dest_rows = neighbours.shape[1]
    picked = jnp.take(columns, neighbours, axis=1)
    counter = relation_counts(relation_ids, 0)
    slabs = [columns[:, :dest_rows]]
    for relation in range(RELATIONS):
        chosen = relation_ids == relation
        summed = jnp.sum(
            jnp.where(chosen[None], picked, jnp.zeros((), picked.dtype)), axis=1, dtype=jnp.float32
        )
        slabs.append((summed / counter[relation][None, :]).astype(jnp.bfloat16))
    return jnp.stack(slabs)


def place_requests(owner_flat, within_flat, batches, capacity):
    edges = owner_flat.shape[0]
    matches = (owner_flat[:, None] == jnp.arange(batches, dtype=jnp.int32)[None, :]).astype(
        jnp.bfloat16
    )
    order = jnp.arange(edges, dtype=jnp.int32)
    earlier = (order[None, :] < order[:, None]).astype(jnp.bfloat16)
    before = jnp.dot(earlier, matches, preferred_element_type=jnp.float32)
    slot_index = jnp.sum(before * matches.astype(jnp.float32), axis=1).astype(jnp.int32)
    places = (slot_index[:, None] == jnp.arange(capacity, dtype=jnp.int32)[None, :]).astype(
        jnp.float32
    )
    valued = matches.astype(jnp.float32) * within_flat.astype(jnp.float32)[:, None]
    request = jnp.einsum("eb,ec->bc", valued, places, precision=lax.Precision.HIGHEST).astype(
        jnp.int32
    )
    return (slot_index, request)


def body(feats, nbr_one, rel_one, w_one, owner_two, local_two, rel_two, w_two):
    columns = feats[0]
    slabs = first_means(columns, nbr_one[0], rel_one[0])
    batches = lax.axis_size("batch")
    capacity = (2 * ROWS * FANOUT_TWO + batches - 1) // batches
    span = batches * capacity
    labels = jnp.arange(RELATIONS * span, dtype=jnp.int32)
    owners = owner_two[0, :, :, 0]
    within = local_two[0]
    relation_ids = rel_two[0]
    portion = slabs
    hidden_one = jax.nn.relu(
        lax.psum_scatter(
            jnp.einsum("sfd,sfh->dh", portion, w_one, preferred_element_type=jnp.float32).astype(
                jnp.bfloat16
            ),
            "feat",
            scatter_dimension=0,
            tiled=True,
        ).astype(jnp.float32)
    ).astype(jnp.bfloat16)
    offset = lax.axis_index("feat") * ROWS
    mine_owner = lax.dynamic_slice_in_dim(owners, offset, ROWS, 0).reshape(-1)
    mine_within = lax.dynamic_slice_in_dim(within, offset, ROWS, 0).reshape(-1)
    mine_ids = lax.dynamic_slice_in_dim(relation_ids, offset, ROWS, 0)
    slot_index, request = place_requests(mine_owner, mine_within, batches, capacity)
    onehot = (
        lax.all_to_all(request, "batch", split_axis=0, concat_axis=0, tiled=True)[..., None]
        == jnp.arange(ROWS, dtype=jnp.int32)
    ).astype(jnp.bfloat16)
    replies = jnp.einsum(
        "bmr,rh->bmh", onehot, hidden_one, preferred_element_type=jnp.float32
    ).astype(jnp.bfloat16)
    arrived = lax.all_to_all(replies, "batch", split_axis=0, concat_axis=0, tiled=True)
    flat = arrived.reshape(span, arrived.shape[2])
    positions = (mine_owner * capacity + slot_index).reshape(ROWS, FANOUT_TWO)
    keys = mine_ids * span + positions
    table = jnp.zeros((ROWS, RELATIONS * span), jnp.bfloat16)
    for slot in range(FANOUT_TWO):
        table = table + (keys[:, slot][:, None] == labels[None, :]).astype(jnp.bfloat16)
    table = table.reshape(ROWS, RELATIONS, span)
    summed = jnp.einsum("drc,ch->rdh", table, flat, preferred_element_type=jnp.float32)
    counter = relation_counts(mine_ids, 1)
    means = (summed / counter[:, :, None]).astype(jnp.bfloat16)
    inputs = jnp.concatenate([hidden_one[None], means], axis=0)
    block_size = w_two.shape[1]
    shard_piece = lax.all_gather(w_two, "feat", axis=1, tiled=True)
    amount = shard_piece.shape[1]
    groups = amount // block_size
    portion = inputs
    portion = portion.reshape(portion.shape[0], portion.shape[1], groups, block_size)
    weights = shard_piece.reshape(shard_piece.shape[0], groups, block_size, shard_piece.shape[2])
    products = jnp.einsum("sdgk,sgkh->gdh", portion, weights, preferred_element_type=jnp.float32)
    rounded = lax.optimization_barrier(products.astype(jnp.bfloat16)).astype(jnp.float32)
    running = jnp.sum(rounded, axis=0)
    result = jax.nn.relu(running).astype(jnp.bfloat16)
    return result[None]


def solution(mesh):
    in_specs = (
        P("batch", "feat", None),
        P("batch", None, None),
        P("batch", None, None),
        P(None, "feat", None),
        P("batch", None, None, None),
        P("batch", None, None),
        P("batch", None, None),
        P(None, "feat", None),
    )
    out_specs = P("batch", "feat", None)
    return jax.shard_map(body, mesh=mesh, in_specs=in_specs, out_specs=out_specs, check_vma=False)
```

profile of v0, /device:TPU:1, one launch (start us, length us, event | category | flops | bytes accessed | tf_op | source)
XLA Modules:
  0.0 303.8 jit_solution(5919092703397115076)
XLA Ops:
  6.5 0.9 compare_select_fusion
  7.5 0.9 compare_and_fusion
  8.4 1.1 broadcast_compare_fusion.1
  9.4 1.1 convert_reduce_fusion.8
  10.6 2.0 copy.27
  12.6 0.9 fusion.45
  13.5 53.9 %gather_fusion = bf16[15360,48]{1,0:T(8,128)(2,1)} fusion(bf16[48,8192]{0,1:T(8,128)(2,1)S(1)} %copy.27, s32[15360]{0:T(1024)S(1)} %broadcast_clamp_fusion), kind=kCustom, calls=%fused_computation | custom fusion | bytes 3010560 | tf_op jit(solution)/shard_map/jit(_take)/gather | solution.py:21
  67.5 13.3 %convert_reduce_fusion = (f32[1024,48]{1,0:T(8,128)S(1)}, f32[1024,48]{1,0:T(8,128)S(1)}, f32[1024,48]{1,0:T(8,128)S(1)}, f32[1024,48]{1,0:T(8,128)S(1)}) fusion(pred[15,1024]{1,0:T(8,128)(4,1)S(1)} %get-tuple-element.41, bf16[15,1024,48]{2,1,0:T(8,128)(2,1)} %bitcast.106, pred[15,1024]{1,0:T(8,128)(4,1)S(1)} %compare_and_fusion, ...), kind=kLoop, calls=%fused_computation.3 | loop fusion | flops 9388032 | bytes 2337792 | tf_op jit(solution)/shard_map/reduce_sum | solution.py:26
  80.8 0.2 copy.28
  81.3 0.2 copy.30
  81.4 0.2 copy.31
  81.7 2.0 bitcast_convert_fusion.1
  83.9 0.7 all-gather.2.cloned.1.call-update
  84.6 0.8 constant_dynamic-slice_fusion.1
  85.6 0.3 fusion.11
  85.9 0.8 dynamic-slice_convert_fusion
  86.9 0.3 convolution_convert_fusion.1
  87.3 16.5 %all_to_all.14 = s32[32,1,40]{2,1,0:T(1,128)S(1)} all-to-all(s32[32,1,40]{2,1,0:T(1,128)S(1)} %bitcast.116), channel_id=1, replica_groups=mesh['feat'=16,'batch'=32] {'batch'}, dimensions={0} | all-to-all | bytes 10240 | tf_op jit(solution)/shard_map/all_to_all | solution.py:79
  103.8 48.3 %reduce-scatter.2.cloned.1.call-done = bf16[64,1024]{1,0:T(8,128)(2,1)} async-done(((bf16[1024,1024]{1,0:T(8,128)(2,1)}), bf16[64,1024]{1,0:T(8,128)(2,1)}) %reduce-scatter.2.cloned.1.call-update) | async-done | bytes 131088 | tf_op jit(solution)/shard_map/reduce_scatter | solution.py:64
  152.1 3.3 %convolution_convert_fusion = bf16[32,40,1024]{2,1,0:T(8,128)(2,1)} fusion(s32[32,40]{1,0:T(8,128)S(1)} %bitcast.111, bf16[64,1024]{1,0:T(8,128)(2,1)} %reduce-scatter.2.cloned.1.call-done), kind=kOutput, calls=%fused_computation.11 | convolution fusion | flops 169361408 | bytes 2757632 | tf_op jit(solution)/shard_map/bmr,rh->bmh/dot_general | solution.py:82
  155.4 18.2 %all-to-all-start.1 = ((bf16[32,40,1024]{2,1,0:T(8,128)(2,1)}), bf16[32,40,1024]{2,1,0:T(8,128)(2,1)S(1)}, u32[]{:S(2)}, u32[]{:S(2)}) async-start(bf16[32,40,1024]{2,1,0:T(8,128)(2,1)} %convolution_convert_fusion), calls=%async_computation.2 | async-start | bytes 5242880 | tf_op jit(solution)/shard_map/all_to_all | solution.py:85
  174.1 1.0 slice_reduce_fusion.9
  175.1 0.2 concatenate.12
  175.3 0.8 copy.36
  176.1 31.1 %all-to-all-done.1 = bf16[32,40,1024]{2,1,0:T(8,128)(2,1)S(1)} async-done(((bf16[32,40,1024]{2,1,0:T(8,128)(2,1)}), bf16[32,40,1024]{2,1,0:T(8,128)(2,1)S(1)}, u32[]{:S(2)}, u32[]{:S(2)}) %all-to-all-start.1) | async-done | bytes 2621472 | tf_op jit(solution)/shard_map/all_to_all | solution.py:85
  207.2 3.2 %fusion.9 = bf16[4,64,1024]{2,1,0:T(8,128)(2,1)} fusion(bf16[1280,1024,1]{1,0,2:T(8,128)(2,1)S(1)} %bitcast.107, s32[4,1280]{1,0:T(4,128)S(1)} %multiply_add_fusion, s32[64]{0:T(128)S(1)} %get-tuple-element.18, s32[64]{0:T(128)S(1)} %get-tuple-element.19, s32[64]{0:T(128)S(1)} %get-tuple-element.20, s32[64]{0:T(128)S(1)} %get-tuple-element.21, ...), kind=kOutput, calls=%fused_computation.29 | convolution fusion | flops 684720128 | bytes 3169792 | tf_op jit(solution)/shard_map/drc,ch->rdh/dot_general | solution.py:93
  210.3 1.8 concatenate.13
  212.1 0.3 copy.37
  212.4 77.2 %all-gather.2.cloned.1.call-done = bf16[5,1024,1024]{2,1,0:T(8,128)(2,1)} async-done(((bf16[5,64,1024]{2,1,0:T(8,128)(2,1)}), bf16[5,1024,1024]{2,1,0:T(8,128)(2,1)}) %all-gather.2.cloned.1.call-update) | async-done | bytes 10485776 | tf_op jit(solution)/shard_map/all_gather | solution.py:98
  289.6 6.3 %bitcast_convert_fusion = bf16[16,64,1024]{2,1,0:T(8,128)(2,1)S(1)} fusion(bf16[5,16,64,1024]{3,2,1,0:T(8,128)(2,1)} %bitcast.121, bf16[4,64,16,64]{3,1,0,2:T(8,128)(2,1)S(1)} %copy.37, bf16[1,64,16,64]{3,1,0,2:T(8,128)(2,1)S(1)} %copy-done.2), kind=kOutput, calls=%fused_computation.7 | convolution fusion | flops 672464896 | bytes 13238272 | tf_op jit(solution)/shard_map/sdgk,sgkh->gdh/dot_general | solution.py:104
  295.9 0.3 convert_reduce_fusion.4
  296.3 0.7 fusion.39
  (37 shorter events, 1.4 us)
Async XLA Ops:
  6.5 75.2 %copy-start = (bf16[5,48,1024]{2,1,0:T(8,128)(2,1)S(1)}, bf16[5,48,1024]{2,1,0:T(8,128)(2,1)}, u32[]{:S(2)}) copy-start(bf16[5,48,1024]{2,1,0:T(8,128)(2,1)} %param.11) | copy-start | bytes 1474564
  6.5 145.6 %reduce-scatter.2.cloned.1.call-start = ((), (), s32[]{:S(2)}) async-start(), calls=%async_computation.3 | async-start | bytes 2228224 | tf_op jit(solution)/shard_map/reduce_scatter | solution.py:64
  83.8 205.8 %all-gather.2.cloned.1.call-start = ((), (), s32[]{:S(2)}) async-start(), calls=%async_computation.4 | async-start | bytes 11141120 | tf_op jit(solution)/shard_map/all_gather | solution.py:98
  155.4 19.6 %copy-start.1 = (bf16[64,1024]{1,0:T(8,128)(2,1)S(1)}, bf16[64,1024]{1,0:T(8,128)(2,1)}, u32[]{:S(2)}) copy-start(bf16[64,1024]{1,0:T(8,128)(2,1)} %reduce-scatter.2.cloned.1.call-done) | copy-start | bytes 393220
  155.4 51.8 %all-to-all-start.1 = ((bf16[32,40,1024]{2,1,0:T(8,128)(2,1)}), bf16[32,40,1024]{2,1,0:T(8,128)(2,1)S(1)}, u32[]{:S(2)}, u32[]{:S(2)}) async-start(bf16[32,40,1024]{2,1,0:T(8,128)(2,1)} %convolution_convert_fusion), calls=%async_computation.2 | async-start | bytes 5242880 | tf_op jit(solution)/shard_map/all_to_all | solution.py:85
  210.3 79.3 %copy-start.2 = (bf16[1,64,16,64]{3,1,0,2:T(8,128)(2,1)S(1)}, bf16[1,64,16,64]{3,1,0,2:T(8,128)(2,1)}, u32[]{:S(2)}) copy-start(bf16[1,64,16,64]{3,1,0,2:T(8,128)(2,1)} %copy.36) | copy-start | bytes 393220
Sparse Core Ops, SparseCore 0:
  83.9 68.0 reduce-scatter.1
  154.2 135.3 all-gather.1
where the time goes:
time: 304 us
  waiting for transfers between devices  157 us (52%)
  local copies, waits for them, and re-layouts  63.1 us (21%)
  other arithmetic  19.5 us (6%)
  starting transfers between devices  18.3 us (6%)
  blocking collectives  16.5 us (5%)
  matrix products  15.5 us (5%)
  between operations  13.7 us (5%)
    all_gather x1, waiting for transfers between devices, body(): shard_piece = lax.all_gather(w_two, 'feat', axis=1, tiled=True)  77.2 us
    gather x1, local copies, waits for them, and re-layouts, first_means(): picked = jnp.take(columns, neighbours, axis=1)  53.9 us
    reduce_scatter x1, waiting for transfers between devices, body(): lax.psum_scatter(jnp.einsum('sfd,sfh->dh', portion, w_one, preferred_elem...  48.3 us
    all_to_all x1, waiting for transfers between devices, body(): lax.all_to_all(replies, 'batch', split_axis=0, concat_axis=0, tiled=True)  31.1 us
    all_to_all x1, starting transfers between devices, body(): lax.all_to_all(replies, 'batch', split_axis=0, concat_axis=0, tiled=True)  18.2 us
    all_to_all x1, blocking collectives, body(): lax.all_to_all(request, 'batch', split_axis=0, concat_axis=0, tiled=True)  16.5 us
    reduce_sum x1, other arithmetic, first_means(): jnp.sum(jnp.where(chosen[None], picked, jnp.zeros((), picked.dtype)), axi...  13.3 us
    dot_general x1, matrix products, body(): jnp.einsum('sdgk,sgkh->gdh', portion, weights, preferred_element_type=jnp...  6.33 us
  transfers between devices with their start and end apart: 3, of which 3 were waited for; matrix products, arithmetic and copies ran while one was open for 4% of the time, Pallas kernels for 0%

commit v1 on v0

v1 whole, which is shorter than its diff:
```python
import jax
import jax.numpy as jnp
from jax import lax
from jax.experimental import pallas as pl
from jax.experimental.pallas import tpu as pltpu
from jax.sharding import PartitionSpec as P

RELATIONS = 4
FANOUT_ONE = 15
FANOUT_TWO = 10
ROWS = 64
LANES = 128


def build_table(feats, table):
    def step(chunk, carry):
        at = pl.multiple_of(chunk * LANES, LANES)
        columns = feats[:, pl.ds(at, LANES)].astype(jnp.float32)
        gap = jnp.zeros((LANES // 2 - columns.shape[0], LANES), jnp.float32)
        table[pl.ds(at, LANES), :] = jnp.concatenate([columns, gap, columns, gap], axis=0).T
        return carry

    lax.fori_loop(0, table.shape[0] // LANES, step, 0, unroll=4)


def build_relations(rel, by_row):
    for chunk in range(by_row.shape[0] // LANES):
        ids = rel[:, chunk * LANES : (chunk + 1) * LANES].astype(jnp.float32)
        ids = jnp.concatenate([ids, jnp.full((1, LANES), 4.0, jnp.float32)], axis=0)
        by_row[chunk * LANES : (chunk + 1) * LANES, :] = ids.T


def eight_means(base, nbr, table, by_row, picked):
    tile = (8, LANES)
    half = (lax.broadcasted_iota(jnp.int32, tile, 1) // 64).astype(jnp.float32)
    ids = by_row[pl.ds(base, 8), :]
    for k in range(FANOUT_ONE):
        for i in range(8):
            picked[k * 8 + i : k * 8 + i + 1, :] = table[pl.ds(nbr[k, base + i], 1), :]
    zero = jnp.zeros(tile, jnp.float32)
    low, high, low_count, high_count = zero, zero, zero, zero
    for k in range(FANOUT_ONE):
        rows = picked[k * 8 : (k + 1) * 8, :]
        own = jnp.broadcast_to(ids[:, k : k + 1], tile)
        in_low, in_high = own == half, own == half + 2.0
        low = low + jnp.where(in_low, rows, 0.0)
        high = high + jnp.where(in_high, rows, 0.0)
        low_count = low_count + jnp.where(in_low, 1.0, 0.0)
        high_count = high_count + jnp.where(in_high, 1.0, 0.0)
    return low / jnp.maximum(low_count, 1.0), high / jnp.maximum(high_count, 1.0)


def aggregate_kernel(nbr, feats, rel, means, own, table, by_row, picked):
    build_table(feats, table)
    build_relations(rel, by_row)

    def step(group, carry):
        at = pl.multiple_of(group * 16, 16)
        pairs = [
            eight_means(at + u * 8, nbr, table, by_row, picked.at[u]) for u in range(2)
        ]
        for side in range(2):
            both = jnp.concatenate([pair[side] for pair in pairs], axis=0)
            means[pl.ds(at, 16), side * LANES : (side + 1) * LANES] = both.astype(jnp.bfloat16)
        return carry

    lax.fori_loop(0, means.shape[0] // 16, step, 0)
    own[...] = table[0 : own.shape[0], :].astype(jnp.bfloat16)


def aggregate(columns, neighbours, relation_ids):
    sources = columns.shape[1]
    dest = neighbours.shape[1]
    vmem = pl.BlockSpec(memory_space=pltpu.VMEM)
    return pl.pallas_call(
        aggregate_kernel,
        out_shape=(
            jax.ShapeDtypeStruct((dest, 2 * LANES), jnp.bfloat16),
            jax.ShapeDtypeStruct((dest, LANES), jnp.bfloat16),
        ),
        in_specs=[pl.BlockSpec(memory_space=pltpu.SMEM), vmem, vmem],
        out_specs=(vmem, vmem),
        scratch_shapes=[
            pltpu.VMEM((sources, LANES), jnp.float32),
            pltpu.VMEM((dest, 16), jnp.float32),
            pltpu.VMEM((2, FANOUT_ONE * 8, LANES), jnp.float32),
        ],
        compiler_params=pltpu.CompilerParams(vmem_limit_bytes=32 << 20),
        cost_estimate=pl.CostEstimate(flops=200_000_000, bytes_accessed=2_000_000, transcendentals=0),
        name="aggregate",
    )(neighbours, columns, relation_ids)


def spread_weights(w_one):
    slabs, depth, width = w_one.shape
    padded = jnp.pad(w_one, ((0, 0), (0, 64 - depth), (0, 0)))
    relation = padded[1:].reshape(RELATIONS * 64, width)
    own = jnp.pad(padded[0], ((0, 64), (0, 0)))
    return relation, own


def body(feats, nbr_one, rel_one, w_one, owner_two, local_two, rel_two, w_two):
    batch_size = lax.axis_size("batch")
    block = w_two.shape[1]
    piece = block // batch_size
    mine = lax.dynamic_slice_in_dim(w_two, lax.axis_index("batch") * piece, piece, 1)
    along = lax.all_gather(mine, "feat", axis=0)
    weights = lax.all_gather(along, "batch", axis=0)

    means, own = aggregate(feats[0], nbr_one[0], rel_one[0])
    relation_w, own_w = spread_weights(w_one)
    partial = jnp.dot(means, relation_w, preferred_element_type=jnp.float32) + jnp.dot(
        own, own_w, preferred_element_type=jnp.float32
    )
    hidden_one = jax.nn.relu(
        lax.psum_scatter(
            partial.astype(jnp.bfloat16), "feat", scatter_dimension=0, tiled=True
        ).astype(jnp.float32)
    ).astype(jnp.bfloat16)
    everyone = lax.all_gather(hidden_one, "batch", axis=0, tiled=True)

    offset = lax.axis_index("feat") * ROWS
    owners = lax.dynamic_slice_in_dim(owner_two[0, :, :, 0], offset, ROWS, 0)
    within = lax.dynamic_slice_in_dim(local_two[0], offset, ROWS, 0)
    ids = lax.dynamic_slice_in_dim(rel_two[0], offset, ROWS, 0)
    span = batch_size * ROWS
    keys = ids * span + owners * ROWS + within
    labels = jnp.arange(RELATIONS * span, dtype=jnp.int32)
    table = jnp.zeros((ROWS, RELATIONS * span), jnp.bfloat16)
    for slot in range(FANOUT_TWO):
        table = table + (keys[:, slot][:, None] == labels[None, :]).astype(jnp.bfloat16)
    table = table.reshape(ROWS, RELATIONS, span)
    counts = jnp.stack(
        [jnp.maximum(jnp.sum((ids == r).astype(jnp.int32), axis=1), 1) for r in range(RELATIONS)]
    ).astype(jnp.float32)
    summed = jnp.einsum("drc,ch->rdh", table, everyone, preferred_element_type=jnp.float32)
    means_two = (summed / counts[:, :, None]).astype(jnp.bfloat16)
    inputs = jnp.concatenate([hidden_one[None], means_two], axis=0)
    groups = inputs.reshape(RELATIONS + 1, ROWS, lax.axis_size("feat"), batch_size, piece)
    running = jnp.einsum("sdfbk,bfskh->dh", groups, weights, preferred_element_type=jnp.float32)
    return jax.nn.relu(running).astype(jnp.bfloat16)[None]


def solution(mesh):
    in_specs = (
        P("batch", "feat", None),
        P("batch", None, None),
        P("batch", None, None),
        P(None, "feat", None),
        P("batch", None, None, None),
        P("batch", None, None),
        P("batch", None, None),
        P(None, "feat", None),
    )
    out_specs = P("batch", "feat", None)
    return jax.shard_map(body, mesh=mesh, in_specs=in_specs, out_specs=out_specs, check_vma=False)
```

time: 304 us -> 280 us (0.921)
  local copies, waits for them, and re-layouts: 63.1 us -> 6.73 us
  Pallas kernels: 0 us -> 25.1 us
  waiting for transfers between devices: 157 us -> 182 us
  starting transfers between devices: 18.3 us -> 0.09 us
  other arithmetic: 19.5 us -> 2.45 us
  blocking collectives: 16.5 us -> 25.6 us
  matrix products: 15.5 us -> 23.9 us
    gather x1 -> x0, local copies, waits for them, and re-layouts: 53.9 us -> none  [first_means(): picked = jnp.take(columns, neighbours, axis=1)]
    all_gather x1 -> x2, waiting for transfers between devices: 77.2 us -> 114 us  [the longest x1 70.3 us: body(): weights = lax.all_gather(along, 'batch', axis=0)]
    all_to_all x1 -> x0, waiting for transfers between devices: 31.1 us -> none  [body(): lax.all_to_all(replies, 'batch', split_axis=0, concat_axis=0, tiled=True)]
    all_gather x0 -> x1, blocking collectives: none -> 25.6 us  [body(): along = lax.all_gather(mine, 'feat', axis=0)]
    pallas_call x0 -> x1, Pallas kernels: none -> 25.1 us  [aggregate(): pl.pallas_call(aggregate_kernel, out_shape=(jax.ShapeDtypeStruct((dest, 2...]
    reduce_scatter x1, waiting for transfers between devices: 48.3 us -> 68.2 us  [body(): lax.psum_scatter(partial.astype(jnp.bfloat16), 'feat', scatter_dimension=...]
    all_to_all x1 -> x0, starting transfers between devices: 18.2 us -> none  [body(): lax.all_to_all(replies, 'batch', split_axis=0, concat_axis=0, tiled=True)]
    all_to_all x1 -> x0, blocking collectives: 16.5 us -> none  [body(): lax.all_to_all(request, 'batch', split_axis=0, concat_axis=0, tiled=True)]
  transfers between devices with their start and end apart: 3 -> 3, of which waited for: 3 -> 3; matrix products, arithmetic and copies ran while one was open for 4% -> 3% of each run, Pallas kernels for 0% -> 0%
where the time goes in v1:
time: 280 us; the launch traced here: 279 us
  waiting for transfers between devices  182 us (65%)
  blocking collectives  25.6 us (9%)
  Pallas kernels  25.1 us (9%)
  matrix products  23.9 us (9%)
  between operations  13.3 us (5%)
  local copies, waits for them, and re-layouts  6.73 us (2%)
    all_gather x1, waiting for transfers between devices, body(): weights = lax.all_gather(along, 'batch', axis=0)  70.3 us
    reduce_scatter x1, waiting for transfers between devices, body(): lax.psum_scatter(partial.astype(jnp.bfloat16), 'feat', scatter_dimension=...  68.2 us
    all_gather x1, waiting for transfers between devices, body(): everyone = lax.all_gather(hidden_one, 'batch', axis=0, tiled=True)  43.3 us
    all_gather x1, blocking collectives, body(): along = lax.all_gather(mine, 'feat', axis=0)  25.6 us
    pallas_call x1, Pallas kernels, aggregate(): pl.pallas_call(aggregate_kernel, out_shape=(jax.ShapeDtypeStruct((dest, 2...  25.1 us
    dot_general x1, matrix products, body(): jnp.einsum('sdfbk,bfskh->dh', groups, weights, preferred_element_type=jnp...  16.5 us
  transfers between devices with their start and end apart: 3, of which 3 were waited for; matrix products, arithmetic and copies ran while one was open for 3% of the time, Pallas kernels for 0%

profile of v1, /device:TPU:1, one launch (start us, length us, event | category | flops | bytes accessed | tf_op | source)
XLA Modules:
  0.0 279.1 jit_solution(12321989653977398152)
XLA Ops:
  6.5 0.0 copy-start
  6.5 0.0 reduce-scatter.2.cloned.1.call-start
  6.5 1.1 pad_slice_fusion.1
  7.6 0.9 fusion.58
  8.6 0.9 copy_bitcast_fusion
  9.4 0.0 copy-start.1
  9.5 1.1 copy-done.1
  10.6 25.1 %aggregate.1 = (bf16[1024,256]{1,0:T(8,128)(2,1)S(1)}, bf16[1024,128]{1,0:T(8,128)(2,1)S(1)}) custom-call(s32[15,1024]{1,0:T(8,128)S(1)} %get-tuple-element.25.nbr, bf16[48,8192]{1,0:T(8,128)(2,1)S(1)} %bitcast.80, s32[15,1024]{1,0:T(8,128)S(1)} %get-tuple-element.24.rel), custom_call_target="tpu_custom_call" | custom-call | flops 200000000 | bytes 2000000 | tf_op jit(solution)/shard_map/aggregate/pallas_call | solution.py:75
  35.7 0.7 fusion.68
  36.4 2.0 add_convert_fusion
  38.5 0.0 reduce-scatter.2.cloned.1.call-update
  38.5 0.0 all-gather.5.cloned.1.call-start
  38.5 68.2 %reduce-scatter.2.cloned.1.call-done = bf16[64,1024]{1,0:T(8,128)(2,1)} async-done(((bf16[1024,1024]{1,0:T(8,128)(2,1)}), bf16[64,1024]{1,0:T(8,128)(2,1)}) %reduce-scatter.2.cloned.1.call-update) | async-done | bytes 131088 | tf_op jit(solution)/shard_map/reduce_scatter | solution.py:116
  106.8 1.6 maximum_convert_fusion
  108.4 0.0 all-gather.5.cloned.1.call-update
  108.4 0.0 all-gather.7.cloned.1.call-start
  108.4 0.0 copy-done
  108.5 25.6 %all-gather = bf16[80,2,1024]{2,1,0:T(2,128)(2,1)} all-gather(bf16[5,2,1024]{2,1,0:T(2,128)(2,1)S(1)} %constant_dynamic-slice_fusion), channel_id=2, replica_groups=mesh['feat'=16,'batch'=32] {'feat'}, dimensions={0}, use_global_device_ids=true | all-gather | bytes 348160 | tf_op jit(solution)/shard_map/all_gather | solution.py:107
  134.1 0.0 all-gather.7.cloned.1.call-update
  134.1 0.8 fusion.62
  135.0 0.8 constant_dynamic-slice_fusion.2
  135.8 1.1 copy.25
  137.0 43.3 %all-gather.5.cloned.1.call-done = bf16[2048,1024]{1,0:T(8,128)(2,1)} async-done(((bf16[64,1024]{1,0:T(8,128)(2,1)}), bf16[2048,1024]{1,0:T(8,128)(2,1)}) %all-gather.5.cloned.1.call-update) | async-done | bytes 4194320 | tf_op jit(solution)/shard_map/all_gather | solution.py:120
  180.3 4.7 %fusion.13 = bf16[4,64,1024]{2,1,0:T(8,128)(2,1)S(1)} fusion(bf16[2048,1024]{1,0:T(8,128)(2,1)} %all-gather.5.cloned.1.call-done, s32[4,2048]{1,0:T(4,128)S(1)} %multiply_add_fusion, s32[64]{0:T(128)S(1)} %get-tuple-element.15, s32[64]{0:T(128)S(1)} %get-tuple-element.16, s32[64]{0:T(128)S(1)} %get-tuple-element.17, s32[64]{0:T(128)S(1)} %get-tuple-element.18, ...), kind=kOutput, calls=%fused_computation.20 | convolution fusion | flops 1095237632 | bytes 4754944 | tf_op jit(solution)/shard_map/drc,ch->rdh/dot_general | solution.py:136
  185.0 0.5 copy.27
  185.5 0.3 copy.29
  185.8 70.3 %all-gather.7.cloned.1.call-done = bf16[512,5,2,1024]{3,2,1,0:T(2,128)(2,1)} async-done(((bf16[16,5,2,1024]{3,2,1,0:T(2,128)(2,1)}), bf16[512,5,2,1024]{3,2,1,0:T(2,128)(2,1)}) %all-gather.7.cloned.1.call-update) | async-done | bytes 10485776 | tf_op jit(solution)/shard_map/all_gather | solution.py:108
  256.1 16.5 %fusion.31 = bf16[1,64,1024]{2,1,0:T(8,128)(2,1)} fusion(bf16[32,16,5,2,1024]{4,3,2,1,0:T(2,128)(2,1)} %bitcast.85, bf16[4,64,16,32,2]{1,3,0,4,2:T(8,128)(2,1)S(1)} %copy.29, bf16[1,64,16,32,2]{1,3,0,4,2:T(8,128)(2,1)S(1)} %copy.28), kind=kOutput, calls=%fused_computation.24 | convolution fusion | flops 671547392 | bytes 11272192 | tf_op jit(solution)/shard_map/sdfbk,bfskh->dh/dot_general | solution.py:140
  (10 shorter events, 0.1 us)
Async XLA Ops:
  6.5 101.9 %copy-start = (bf16[5,64,1024]{2,1,0:T(8,128)(2,1)S(1)}, bf16[5,64,1024]{2,1,0:T(8,128)(2,1)}, u32[]{:S(2)}) copy-start(bf16[5,64,1024]{2,1,0:T(8,128)(2,1)} %param.15) | copy-start | bytes 1966084
  6.5 100.2 %reduce-scatter.2.cloned.1.call-start = ((), (), s32[]{:S(2)}) async-start(), calls=%async_computation.1 | async-start | bytes 2228224 | tf_op jit(solution)/shard_map/reduce_scatter | solution.py:116
  9.4 1.1 copy-start.1
  38.5 141.8 %all-gather.5.cloned.1.call-start = ((), (), s32[]{:S(2)}) async-start(), calls=%async_computation.2 | async-start | bytes 4325376 | tf_op jit(solution)/shard_map/all_gather | solution.py:120
  108.4 147.7 %all-gather.7.cloned.1.call-start = ((), (), s32[]{:S(2)}) async-start(), calls=%async_computation.3 | async-start | bytes 10813440 | tf_op jit(solution)/shard_map/all_gather | solution.py:108
Sparse Core Ops, SparseCore 0:
  38.6 68.1 reduce-scatter.1
  109.9 70.2 all-gather.4
  183.4 72.6 all-gather.6

commit v2 on v1

v2 whole, which is shorter than its diff:
```python
import functools

import jax
import jax.numpy as jnp
from jax import lax
from jax.experimental import pallas as pl
from jax.experimental.pallas import tpu as pltpu
from jax.sharding import PartitionSpec as P

RELATIONS = 4
FANOUT_ONE = 15
FANOUT_TWO = 10
ROWS = 64
LANES = 128
WIDTH = 1024
HALF = WIDTH // 2
FEAT = 16
SIDE = 4
BATCHES = 32
BF16 = jnp.bfloat16
F32 = jnp.float32


class Links:
    def __init__(self, send_sems, recv_sems, anyone):
        self.send_sems, self.recv_sems, self.anyone = send_sems, recv_sems, anyone
        self.count = 0
        self.sent = []

    def _copy(self, index, src, dst, device):
        return pltpu.make_async_remote_copy(
            src_ref=src,
            dst_ref=dst,
            send_sem=self.send_sems.at[index],
            recv_sem=self.recv_sems.at[index],
            device_id=device,
            device_id_type=pl.DeviceIdType.MESH,
        )

    def send(self, ref, device, to=None):
        index = self.count
        self.count += 1
        copy = self._copy(index, ref, ref if to is None else to, device)
        copy.start()
        self.sent.append(copy)
        return index

    def arrive(self, index, ref):
        self._copy(index, ref, ref, self.anyone).wait_recv()

    def finish(self):
        for copy in self.sent:
            copy.wait_send()


def build_table(feats, table, first, last):
    def step(chunk, carry):
        at = pl.multiple_of(chunk * LANES, LANES)
        columns = feats[:, pl.ds(at, LANES)].astype(F32)
        gap = jnp.zeros((LANES // 2 - columns.shape[0], LANES), F32)
        table[pl.ds(at, LANES), :] = jnp.concatenate([columns, gap, columns, gap], axis=0).T
        return carry

    lax.fori_loop(first, last, step, 0, unroll=4)


def build_relations(rel, by_row):
    for chunk in range(by_row.shape[0] // LANES):
        ids = rel[:, chunk * LANES : (chunk + 1) * LANES].astype(F32)
        ids = jnp.concatenate([ids, jnp.full((1, LANES), 4.0, F32)], axis=0)
        by_row[chunk * LANES : (chunk + 1) * LANES, :] = ids.T


def eight_means(base, nbr, table, by_row, picked):
    tile = (8, LANES)
    half = (lax.broadcasted_iota(jnp.int32, tile, 1) // 64).astype(F32)
    ids = by_row[pl.ds(base, 8), :]
    for k in range(FANOUT_ONE):
        for i in range(8):
            picked[k * 8 + i : k * 8 + i + 1, :] = table[pl.ds(nbr[k, base + i], 1), :]
    zero = jnp.zeros(tile, F32)
    low, high, low_count, high_count = zero, zero, zero, zero
    for k in range(FANOUT_ONE):
        rows = picked[k * 8 : (k + 1) * 8, :]
        own = jnp.broadcast_to(ids[:, k : k + 1], tile)
        in_low, in_high = own == half, own == half + 2.0
        low = low + jnp.where(in_low, rows, 0.0)
        high = high + jnp.where(in_high, rows, 0.0)
        low_count = low_count + jnp.where(in_low, 1.0, 0.0)
        high_count = high_count + jnp.where(in_high, 1.0, 0.0)
    return low / jnp.maximum(low_count, 1.0), high / jnp.maximum(high_count, 1.0)


def gather_block(block, row, nbr, table, by_row, picked, slabs):
    def step(group, carry):
        at = pl.multiple_of(group * 16, 16)
        base = pl.multiple_of(block * ROWS + at, 16)
        pairs = [
            eight_means(base + u * 8, nbr, table, by_row, picked.at[u]) for u in range(2)
        ]
        for side in range(2):
            both = jnp.concatenate([pair[side] for pair in pairs], axis=0)
            slabs[pl.ds(row + at, 16), side * LANES : (side + 1) * LANES] = both.astype(BF16)
        return carry

    lax.fori_loop(0, ROWS // 16, step, 0)
    start = pl.multiple_of(block * ROWS, ROWS)
    slabs[row : row + ROWS, 2 * LANES :] = table[pl.ds(start, ROWS), :].astype(BF16)


def kernel(
    nbr,
    feats,
    rel,
    w_one,
    counts,
    scale,
    w_two,
    out,
    table,
    by_row,
    picked,
    slabs,
    weights,
    hidden,
    send_right,
    send_left,
    from_left,
    from_right,
    summed,
    result,
    send_sems,
    recv_sems,
    local_sem,
):
    z = lax.axis_index("feat")
    place = lax.axis_index("batch")
    core = lax.rem(place, 2)
    x = lax.rem(place // 2, SIDE)
    y = place // (2 * SIDE)
    u = x + core * (y - x)
    v = y + core * (x - y)

    def along(offset):
        return lax.rem(z + (FEAT + offset), FEAT)

    def turn(value, offset):
        return lax.rem(value + (SIDE + offset), SIDE)

    def in_plane(u_at, v_at):
        return (z, v_at * (8 - 6 * core) + u_at * (2 + 6 * core) + core)

    right, left = (along(1), place), (along(-1), place)
    u_next, u_prev = in_plane(turn(u, 1), v), in_plane(turn(u, -1), v)
    v_next, v_prev = in_plane(u, turn(v, 1)), in_plane(u, turn(v, -1))
    peer = (z, place + 1 - 2 * core)

    barrier = pltpu.get_barrier_semaphore()
    neighbours = (right, left, u_next, u_prev, v_next, v_prev, peer)
    for device in neighbours:
        pl.semaphore_signal(barrier, inc=1, device_id=device, device_id_type=pl.DeviceIdType.MESH)
    local = pltpu.make_async_copy(w_two, weights.at[:, z], local_sem)
    local.start()
    build_relations(rel, by_row)
    build_table(feats, table, 0, 16)
    local.wait()
    pl.semaphore_wait(barrier, len(neighbours))

    links = Links(send_sems, recv_sems, peer)

    def piece(f, u_at):
        return weights.at[:, f, v, :, pl.ds(pl.multiple_of((core * SIDE + u_at) * LANES, LANES), LANES)]

    def stripe(f, v_at):
        return weights.at[:, f, v_at, :, pl.ds(pl.multiple_of(core * HALF, HALF), HALF)]

    def column_half(f, which):
        return weights.at[:, f, :, :, pl.ds(pl.multiple_of(which * HALF, HALF), HALF)]

    z_sent, one, one_far, two, two_far, across = {}, {}, {}, {}, {}, {}

    def sides(t):
        return (-1, 1) if t < FEAT // 2 else (-1,)

    def z_step(t):
        for side in sides(t):
            device = right if side < 0 else left
            z_sent[t, side] = links.send(piece(along(side * (t - 1)), u), device)

    def z_arrive(t):
        for side in sides(t):
            links.arrive(z_sent[t, side], piece(along(side * t), u))

    def one_step(t):
        for side in sides(t):
            f = along(side * t)
            one[t, side] = (links.send(piece(f, u), u_next), links.send(piece(f, u), u_prev))

    def one_far_step(t):
        for side in sides(t):
            f = along(side * t)
            links.arrive(one[t, side][0], piece(f, turn(u, -1)))
            links.arrive(one[t, side][1], piece(f, turn(u, 1)))
            if side < 0:
                one_far[t, side] = links.send(piece(f, turn(u, -1)), u_next)
            else:
                one_far[t, side] = links.send(piece(f, turn(u, 1)), u_prev)

    def two_step(t):
        for side in sides(t):
            f = along(side * t)
            links.arrive(one_far[t, side], piece(f, turn(u, 2)))
            two[t, side] = (links.send(stripe(f, v), v_next), links.send(stripe(f, v), v_prev))

    def two_far_step(t):
        for side in sides(t):
            f = along(side * t)
            links.arrive(two[t, side][0], stripe(f, turn(v, -1)))
            links.arrive(two[t, side][1], stripe(f, turn(v, 1)))
            if side < 0:
                two_far[t, side] = links.send(stripe(f, turn(v, -1)), v_next)
            else:
                two_far[t, side] = links.send(stripe(f, turn(v, 1)), v_prev)

    def across_step(t):
        for side in sides(t):
            f = along(side * t)
            links.arrive(two_far[t, side], stripe(f, turn(v, 2)))
            across[t, side] = links.send(column_half(f, core), peer)

    steps = FEAT // 2

    def serve(slot):
        if 1 <= slot <= steps:
            z_arrive(slot)
            if slot < steps:
                z_step(slot + 1)
        for lag, action in enumerate((one_step, one_far_step, two_step, two_far_step, across_step)):
            t, odd = divmod(slot - lag, 2)
            if not odd and 1 <= t <= steps:
                action(t)

    z_step(1)
    for quarter in range(1, 4):
        build_table(feats, table, 16 * quarter, 16 * quarter + 16)
        serve(quarter)

    in_right, in_left = {}, {}
    slot = 4
    for s in range(steps + 1):
        gather_block(along(steps - s), 0, nbr, table, by_row, picked, slabs)
        serve(slot)
        slot += 1
        if 0 < s < steps:
            gather_block(along(s - steps), ROWS, nbr, table, by_row, picked, slabs)
        serve(slot)
        slot += 1
        rows = 2 * ROWS if 0 < s < steps else ROWS
        for h in range(2):
            columns = slice(h * HALF, (h + 1) * HALF)
            partial = jnp.dot(slabs[0:rows, :], w_one[:, columns], preferred_element_type=F32)
            if s == 0:
                if h == 0:
                    send_right[0, 0] = partial.astype(BF16)
                    in_right[0, 0] = links.send(send_right.at[0, 0], right, from_left.at[0, 0])
                else:
                    send_left[0, 1] = partial.astype(BF16)
                    in_left[0, 1] = links.send(send_left.at[0, 1], left, from_right.at[0, 1])
                continue
            if s == steps:
                links.arrive(in_right[s - 1, h], from_left.at[s - 1, h])
                links.arrive(in_left[s - 1, h], from_right.at[s - 1, h])
                total = partial + from_left[s - 1, h].astype(F32) + from_right[s - 1, h].astype(F32)
                hidden[core, v, u, :, columns] = jnp.maximum(total, 0.0).astype(BF16)
                continue
            onward, back = partial[:ROWS], partial[ROWS:]
            if (s - 1, h) in in_right:
                links.arrive(in_right[s - 1, h], from_left.at[s - 1, h])
                onward = onward + from_left[s - 1, h].astype(F32)
            send_right[s, h] = onward.astype(BF16)
            in_right[s, h] = links.send(send_right.at[s, h], right, from_left.at[s, h])
            if (s - 1, h) in in_left:
                links.arrive(in_left[s - 1, h], from_right.at[s - 1, h])
                back = back + from_right[s - 1, h].astype(F32)
            send_left[s, h] = back.astype(BF16)
            in_left[s, h] = links.send(send_left.at[s, h], left, from_right.at[s, h])

    def rows_of(du, dv, part=None):
        ref = hidden.at[core, turn(v, dv), turn(u, du)]
        if part is None:
            return ref
        return ref.at[pl.ds(part * (ROWS // 2), ROWS // 2)]

    def rows_of_peer(du, dv):
        return hidden.at[1 - core, turn(u, dv), turn(v, du)]

    u_direct = (links.send(rows_of(0, 0), u_next), links.send(rows_of(0, 0), u_prev))
    v_direct, v_far, crossed = {}, {}, {}

    def cross(du, dv):
        crossed[du, dv] = links.send(rows_of(du, dv), peer)

    def v_send(du):
        v_direct[du] = (links.send(rows_of(du, 0), v_next), links.send(rows_of(du, 0), v_prev))

    def v_forward(du):
        links.arrive(v_direct[du][0], rows_of(du, -1))
        links.arrive(v_direct[du][1], rows_of(du, 1))
        v_far[du] = (
            links.send(rows_of(du, -1, 0), v_next),
            links.send(rows_of(du, 1, 1), v_prev),
        )
        cross(du, -1)
        cross(du, 1)

    def v_arrive_far(du):
        links.arrive(v_far[du][0], rows_of(du, 2, 0))
        links.arrive(v_far[du][1], rows_of(du, 2, 1))
        cross(du, 2)

    def add_group(which, v_at, first=False):
        group = which * SIDE + v_at
        columns = pl.ds(pl.multiple_of(group * 2 * LANES, 2 * LANES), 2 * LANES)

        def step(n, carry):
            at = pl.ds(pl.multiple_of(n * 256, 256), 256)
            rows = hidden[which, v_at, :, :, at].reshape(SIDE * ROWS, 256)
            product = jnp.dot(counts[:, columns], rows, preferred_element_type=F32)
            summed[:, at] = product if first else summed[:, at] + product
            return carry

        lax.fori_loop(0, WIDTH // 256, step, 0)

    def times_weights(slab, left_rows, first=False):
        def step(n, carry):
            at = pl.ds(pl.multiple_of(n * 256, 256), 256)
            w = weights[slab, :, :, :, at].reshape(WIDTH, 256)
            product = jnp.dot(left_rows, w, preferred_element_type=F32)
            result[:, at] = product if first else result[:, at] + product
            return carry

        lax.fori_loop(0, WIDTH // 256, step, 0)

    v_send(0)
    cross(0, 0)
    links.arrive(u_direct[0], rows_of(-1, 0))
    links.arrive(u_direct[1], rows_of(1, 0))
    u_far = (links.send(rows_of(-1, 0, 0), u_next), links.send(rows_of(1, 0, 1), u_prev))
    v_send(-1)
    v_send(1)
    cross(-1, 0)
    cross(1, 0)
    v_forward(0)
    links.arrive(u_far[0], rows_of(2, 0, 0))
    links.arrive(u_far[1], rows_of(2, 0, 1))
    v_send(2)
    cross(2, 0)
    add_group(core, v, first=True)
    v_forward(-1)
    v_forward(1)
    v_arrive_far(0)
    for t in range(1, steps + 1):
        for side in sides(t):
            links.arrive(across[t, side], column_half(along(side * t), 1 - core))
    times_weights(0, hidden[core, v, u], first=True)
    for du in (0, -1, 1, 2):
        links.arrive(crossed[du, 0], rows_of_peer(du, 0))
    add_group(1 - core, u)
    v_forward(2)
    v_arrive_far(-1)
    v_arrive_far(1)
    for dv in (-1, 1):
        add_group(core, turn(v, dv))
    v_arrive_far(2)
    for dv in (-1, 1):
        for du in (0, -1, 1, 2):
            links.arrive(crossed[du, dv], rows_of_peer(du, dv))
        add_group(1 - core, turn(u, dv))
    add_group(core, turn(v, 2))
    for du in (0, -1, 1, 2):
        links.arrive(crossed[du, 2], rows_of_peer(du, 2))
    add_group(1 - core, turn(u, 2))

    for r in range(RELATIONS):
        mean = summed[r * ROWS : (r + 1) * ROWS, :] / scale[r * ROWS : (r + 1) * ROWS, :]
        times_weights(r + 1, mean.astype(BF16))
    out[...] = jnp.maximum(result[...], 0.0).astype(BF16)
    links.finish()


COPIES = 192


def two_layers(nbr, feats, rel, w_one, counts, scale, w_two):
    sources = feats.shape[1]
    dest = nbr.shape[1]
    vmem = pl.BlockSpec(memory_space=pltpu.VMEM)
    half_steps = FEAT // 2
    travelling = pltpu.VMEM((half_steps, 2, ROWS, HALF), BF16)
    return pl.pallas_call(
        kernel,
        out_shape=jax.ShapeDtypeStruct((ROWS, WIDTH), BF16),
        in_specs=[pl.BlockSpec(memory_space=pltpu.SMEM)]
        + [vmem] * 5
        + [pl.BlockSpec(memory_space=pl.ANY)],
        out_specs=vmem,
        scratch_shapes=[
            pltpu.VMEM((sources, LANES), F32),
            pltpu.VMEM((dest, 16), F32),
            pltpu.VMEM((2, FANOUT_ONE * 8, LANES), F32),
            pltpu.VMEM((2 * ROWS, 3 * LANES), BF16),
            pltpu.VMEM((RELATIONS + 1, FEAT, SIDE, ROWS // SIDE, WIDTH), BF16),
            pltpu.VMEM((2, SIDE, SIDE, ROWS, WIDTH), BF16),
            travelling,
            travelling,
            travelling,
            travelling,
            pltpu.VMEM((RELATIONS * ROWS, WIDTH), F32),
            pltpu.VMEM((ROWS, WIDTH), F32),
            pltpu.SemaphoreType.DMA((COPIES + 32,)),
            pltpu.SemaphoreType.DMA((COPIES + 32,)),
            pltpu.SemaphoreType.DMA,
        ],
        compiler_params=pltpu.CompilerParams(
            vmem_limit_bytes=48 << 20, collective_id=0, has_side_effects=True
        ),
        cost_estimate=pl.CostEstimate(
            flops=2_400_000_000, bytes_accessed=4_000_000, transcendentals=0
        ),
        name="two_layers",
    )(nbr, feats, rel, w_one, counts, scale, w_two)


def spread_weights(w_one):
    padded = jnp.pad(w_one, ((0, 0), (0, 64 - w_one.shape[1]), (0, 0)))
    relation = padded[1:].reshape(RELATIONS * 64, w_one.shape[2])
    return jnp.concatenate([relation, padded[0], jnp.zeros_like(padded[0])], axis=0)


def count_table(owner_two, local_two, rel_two):
    offset = lax.axis_index("feat") * ROWS
    owners = lax.dynamic_slice_in_dim(owner_two, offset, ROWS, 0)
    within = lax.dynamic_slice_in_dim(local_two, offset, ROWS, 0)
    ids = lax.dynamic_slice_in_dim(rel_two, offset, ROWS, 0)
    core, x, y = owners % 2, (owners // 2) % SIDE, owners // (2 * SIDE)
    held = jnp.where(core == 0, y * SIDE + x, SIDE * SIDE + x * SIDE + y)
    span = BATCHES * ROWS
    keys = ids * span + held * ROWS + within
    labels = jnp.arange(RELATIONS * span, dtype=jnp.int32)
    table = jnp.zeros((ROWS, RELATIONS * span), BF16)
    for slot in range(FANOUT_TWO):
        table = table + (keys[:, slot][:, None] == labels[None, :]).astype(BF16)
    table = table.reshape(ROWS, RELATIONS, span).transpose(1, 0, 2).reshape(RELATIONS * ROWS, span)
    counted = jnp.stack(
        [jnp.maximum(jnp.sum((ids == r).astype(jnp.int32), axis=1), 1) for r in range(RELATIONS)]
    ).astype(F32)
    return table, counted.reshape(RELATIONS * ROWS, 1)


def body(feats, nbr_one, rel_one, w_one, owner_two, local_two, rel_two, w_two):
    counts, scale = count_table(owner_two[0, :, :, 0], local_two[0], rel_two[0])
    pieces = w_two.reshape(RELATIONS + 1, SIDE, ROWS // SIDE, WIDTH)
    out = two_layers(nbr_one[0], feats[0], rel_one[0], spread_weights(w_one), counts, scale, pieces)
    return out[None]


def solution(mesh):
    in_specs = (
        P("batch", "feat", None),
        P("batch", None, None),
        P("batch", None, None),
        P(None, "feat", None),
        P("batch", None, None, None),
        P("batch", None, None),
        P("batch", None, None),
        P(None, "feat", None),
    )
    out_specs = P("batch", "feat", None)
    return jax.shard_map(body, mesh=mesh, in_specs=in_specs, out_specs=out_specs, check_vma=False)
```

time: 280 us -> 123 us (0.44)
  waiting for transfers between devices: 182 us -> 0 us
  Pallas kernels: 25.1 us -> 115 us
  blocking collectives: 25.6 us -> 0 us
  matrix products: 23.9 us -> 0 us
  between operations: 13.3 us -> 0.16 us
    all_gather x2 -> x0, waiting for transfers between devices: 114 us -> none  [the longest x1 70.3 us: body(): weights = lax.all_gather(along, 'batch', axis=0)]
    pallas_call x1, Pallas kernels: 25.1 us -> 115 us  [two_layers(): pl.pallas_call(kernel, out_shape=jax.ShapeDtypeStruct((ROWS, WIDTH), BF16...]
    reduce_scatter x1 -> x0, waiting for transfers between devices: 68.2 us -> none  [body(): lax.psum_scatter(partial.astype(jnp.bfloat16), 'feat', scatter_dimension=...]
    all_gather x1 -> x0, blocking collectives: 25.6 us -> none  [body(): along = lax.all_gather(mine, 'feat', axis=0)]
    dot_general x4 -> x0, matrix products: 23.9 us -> none  [the longest x1 16.5 us: body(): jnp.einsum('sdfbk,bfskh->dh', groups, weights, preferred_element_type=jnp...]
  transfers between devices with their start and end apart: 3 -> 0, of which waited for: 3 -> 0; matrix products, arithmetic and copies ran while one was open for 3% -> 0% of each run, Pallas kernels for 0% -> 0%
where the time goes in v2:
time: 123 us
  Pallas kernels  115 us (93%)
  local copies, waits for them, and re-layouts  4.36 us (4%)
  other arithmetic  3.36 us (3%)
    pallas_call x1, Pallas kernels, two_layers(): pl.pallas_call(kernel, out_shape=jax.ShapeDtypeStruct((ROWS, WIDTH), BF16...  115 us

profile of v2, /device:TPU:1, one launch (start us, length us, event | category | flops | bytes accessed | tf_op | source)
XLA Modules:
  0.0 122.9 jit_solution(3595197890132117901)
XLA Ops:
  0.0 0.0 copy-start
  0.0 0.0 copy-start.3
  0.0 0.1 pad.11.clone
  0.1 0.7 copy-done
  0.8 0.1 constant_dynamic-slice_fusion.1
  0.9 0.8 fusion.26
  1.8 0.1 eq.310
  1.9 0.1 eq.360
  2.0 0.1 eq.355
  2.1 0.1 eq.350
  2.1 0.1 eq.345
  2.2 0.1 eq.340
  2.3 0.1 eq.335
  2.4 0.1 eq.330
  2.5 0.1 eq.325
  2.6 0.1 eq.320
  2.7 0.1 convert_element_type.107.scale
  2.8 0.9 fusion.19
  3.7 0.9 copy_bitcast_fusion
  4.6 0.0 copy-done.3
  4.7 0.0 copy-start.1
  4.7 0.0 copy-start.2
  4.7 0.2 maximum_maximum_fusion.w_one
  4.9 2.3 %fusion.10.counts = bf16[256,2048]{1,0:T(8,128)(2,1)S(1)} fusion(s32[256]{0:T(256)S(1)} %eq.360, s32[256]{0:T(256)S(1)} %eq.355, s32[256]{0:T(256)S(1)} %eq.350, s32[256]{0:T(256)S(1)} %eq.345, s32[256]{0:T(256)S(1)} %eq.340, s32[256]{0:T(256)S(1)} %eq.335, s32[256]{0:T(256)S(1)} %eq.330, s32[256]{0:T(256)S(1)} %eq.325, s32[256]{0:T(256)S(1)} %eq.320, ...), kind=kLoop, calls=%fused_computation.20 | loop fusion | flops 15204352 | bytes 1091584 | tf_op jit(solution)/shard_map/add | solution.py:452
  7.2 0.0 copy-done.1
  7.2 0.0 copy-done.2
  7.2 115.0 %two_layers.1 = bf16[64,1024]{1,0:T(8,128)(2,1)S(1)} custom-call(s32[15,1024]{1,0:T(8,128)S(1)} %get-tuple-element.22.nbr, bf16[48,8192]{1,0:T(8,128)(2,1)S(1)} %bitcast.140, s32[15,1024]{1,0:T(8,128)S(1)} %get-tuple-element.21.rel, bf16[384,1024]{1,0:T(8,128)(2,1)S(1)} %maximum_maximum_fusion.w_one, bf16[256,2048]{1,0:T(8,128)(2,1)S(1)} %fusion.10.counts, ...), custom_call_target="tpu_custom_call" | custom-call | flops 2400000000 | bytes 4000000 | tf_op jit(solution)/shard_map/two_layers/pallas_call | solution.py:400
  122.2 0.7 copy.47
  (20 shorter events, 0.1 us)
Async XLA Ops:
  0.0 0.8 copy-start
  0.0 4.6 %copy-start.3 = (bf16[5,48,1024]{2,1,0:T(8,128)(2,1)S(1)}, bf16[5,48,1024]{2,1,0:T(8,128)(2,1)}, u32[]{:S(2)}) copy-start(bf16[5,48,1024]{2,1,0:T(8,128)(2,1)} %param.11) | copy-start | bytes 1474564
  4.7 2.5 %copy-start.1 = (bf16[1,48,8192]{2,1,0:T(8,128)(2,1)S(1)}, bf16[1,48,8192]{2,1,0:T(8,128)(2,1)}, u32[]{:S(2)}) copy-start(bf16[1,48,8192]{2,1,0:T(8,128)(2,1)} %param.8) | copy-start | bytes 2359300
  4.7 2.5 %copy-start.2 = (bf16[5,64,1024]{2,1,0:T(8,128)(2,1)S(1)}, bf16[5,64,1024]{2,1,0:T(8,128)(2,1)}, u32[]{:S(2)}) copy-start(bf16[5,64,1024]{2,1,0:T(8,128)(2,1)} %param.15) | copy-start | bytes 1966084

commit v3 on v2

v3 whole, which is shorter than its diff:
```python
import jax
import jax.numpy as jnp
from jax import lax
from jax.experimental import pallas as pl
from jax.experimental.pallas import tpu as pltpu
from jax.sharding import PartitionSpec as P

RELATIONS = 4
FANOUT_ONE = 15
FANOUT_TWO = 10
ROWS = 64
LANES = 128
WIDTH = 1024
HALF = WIDTH // 2
FEAT = 16
SIDE = 4
BATCHES = 32
DEST_ROWS = 8
BF16 = jnp.bfloat16
F32 = jnp.float32


class Links:
    def __init__(self, send_sems, recv_sems, anyone):
        self.send_sems, self.recv_sems, self.anyone = send_sems, recv_sems, anyone
        self.count = 0
        self.sent = []

    def _copy(self, index, src, dst, device):
        return pltpu.make_async_remote_copy(
            src_ref=src,
            dst_ref=dst,
            send_sem=self.send_sems.at[index],
            recv_sem=self.recv_sems.at[index],
            device_id=device,
            device_id_type=pl.DeviceIdType.MESH,
        )

    def send(self, ref, device, to=None):
        index = self.count
        assert index < COPIES
        self.count += 1
        copy = self._copy(index, ref, ref if to is None else to, device)
        copy.start()
        self.sent.append(copy)
        return index

    def arrive(self, index, ref):
        self._copy(index, ref, ref, self.anyone).wait_recv()

    def finish(self):
        for copy in self.sent:
            copy.wait_send()


def build_table(feats, table, first, last):
    def step(chunk, carry):
        at = pl.multiple_of(chunk * LANES, LANES)
        columns = feats[:, pl.ds(at, LANES)].astype(F32)
        gap = jnp.zeros((LANES // 2 - columns.shape[0], LANES), F32)
        table[pl.ds(at, LANES), :] = jnp.concatenate([columns, gap, columns, gap], axis=0).T
        return carry

    lax.fori_loop(first, last, step, 0, unroll=4)


def as_columns(rows):
    rows = rows.astype(F32)
    left = jnp.full((16 - rows.shape[0], LANES), float(RELATIONS), F32)
    return jnp.concatenate([rows, left], axis=0).T


def build_relations(rel, by_row):
    for chunk in range(by_row.shape[0] // LANES):
        by_row[chunk * LANES : (chunk + 1) * LANES, :] = as_columns(rel[:, chunk, :])


def eight_means(base, row, column, nbr, table, by_row, picked):
    tile = (8, LANES)
    half = (lax.broadcasted_iota(jnp.int32, tile, 1) // 64).astype(F32)
    ids = by_row[pl.ds(base, 8), :]
    for k in range(FANOUT_ONE):
        for i in range(8):
            source = nbr[k, row, column + i]
            picked[k * 8 + i : k * 8 + i + 1, :] = table[pl.ds(source, 1), :]
    zero = jnp.zeros(tile, F32)
    low, high, low_count, high_count = zero, zero, zero, zero
    for k in range(FANOUT_ONE):
        rows = picked[k * 8 : (k + 1) * 8, :]
        own = jnp.broadcast_to(ids[:, k : k + 1], tile)
        in_low, in_high = own == half, own == half + 2.0
        low = low + jnp.where(in_low, rows, 0.0)
        high = high + jnp.where(in_high, rows, 0.0)
        low_count = low_count + jnp.where(in_low, 1.0, 0.0)
        high_count = high_count + jnp.where(in_high, 1.0, 0.0)
    return low / jnp.maximum(low_count, 1.0), high / jnp.maximum(high_count, 1.0)


def gather_block(block, to, nbr, table, by_row, picked, slabs):
    row, start = block // 2, lax.rem(block, 2) * ROWS

    def step(group, carry):
        at = pl.multiple_of(group * 16, 16)
        base = pl.multiple_of(block * ROWS + at, 16)
        pairs = [
            eight_means(base + n * 8, row, start + at + n * 8, nbr, table, by_row, picked.at[n])
            for n in range(2)
        ]
        for side in range(2):
            both = jnp.concatenate([pair[side] for pair in pairs], axis=0)
            slabs[pl.ds(to + at, 16), side * LANES : (side + 1) * LANES] = both.astype(BF16)
        return carry

    lax.fori_loop(0, ROWS // 16, step, 0)
    first = pl.multiple_of(block * ROWS, ROWS)
    slabs[to : to + ROWS, 2 * LANES :] = table[pl.ds(first, ROWS), :].astype(BF16)


def build_counts(keys, counts):
    span = counts.shape[1]

    def some_rows(n, carry):
        at = pl.multiple_of(n * 16, 16)
        key = keys[pl.ds(at, 16), :]
        spread = [jnp.broadcast_to(key[:, k : k + 1], (16, LANES)) for k in range(FANOUT_TWO)]
        lane = lax.broadcasted_iota(jnp.int32, (16, LANES), 1).astype(F32)
        for r in range(RELATIONS):
            for c in range(span // LANES):
                label = lane + float(r * span + c * LANES)
                total = jnp.zeros((16, LANES), F32)
                for k in range(FANOUT_TWO):
                    total = total + jnp.where(spread[k] == label, 1.0, 0.0)
                rows = pl.ds(r * ROWS + at, 16)
                counts[rows, c * LANES : (c + 1) * LANES] = total.astype(BF16)
        return carry

    lax.fori_loop(0, ROWS // 16, some_rows, 0)


def kernel(
    nbr_hbm,
    feats_hbm,
    rel_hbm,
    w_one_hbm,
    owner_hbm,
    within_hbm,
    ids_hbm,
    w_two,
    out,
    nbr,
    feats,
    rel,
    w_one,
    two,
    table,
    by_row,
    picked,
    slabs,
    keys,
    ids_two,
    counts,
    weights,
    hidden,
    send_right,
    send_left,
    from_left,
    from_right,
    summed,
    result,
    send_sems,
    recv_sems,
    local_sems,
):
    z = lax.axis_index("feat")
    place = lax.axis_index("batch")
    core = lax.rem(place, 2)
    x = lax.rem(place // 2, SIDE)
    y = place // (2 * SIDE)
    u = x + core * (y - x)
    v = y + core * (x - y)
    z_high, z_low = z // SIDE, lax.rem(z, SIDE)

    def along(offset):
        return lax.rem(z + (FEAT + offset), FEAT)

    def turn(value, offset):
        return lax.rem(value + (SIDE + offset), SIDE)

    def in_plane(u_at, v_at):
        return (z, v_at * (8 - 6 * core) + u_at * (2 + 6 * core) + core)

    z_by = {d: (along(d), place) for d in (1, -1, 2, -2, 4, -4, 8)}
    u_by = {d: in_plane(turn(u, d), v) for d in (1, -1, 2)}
    v_by = {d: in_plane(u, turn(v, d)) for d in (1, -1, 2)}
    right, left = z_by[1], z_by[-1]
    peer = (z, place + 1 - 2 * core)

    def own_columns(u_at):
        return pl.ds(pl.multiple_of((core * SIDE + u_at) * LANES, LANES), LANES)

    chunks = 4
    span = feats.shape[1] // chunks
    copies = [
        (feats_hbm.at[:, pl.ds(n * span, span)], feats.at[:, pl.ds(n * span, span)])
        for n in range(chunks)
    ] + [
        (w_two.at[:, v, :, own_columns(u)], weights.at[:, z_high, z_low, v, :, own_columns(u)]),
        (nbr_hbm, nbr),
        (rel_hbm, rel),
        (w_one_hbm.at[pl.ds(1, RELATIONS)], w_one.at[pl.ds(0, RELATIONS), pl.ds(0, 48)]),
        (w_one_hbm.at[pl.ds(0, 1)], w_one.at[pl.ds(RELATIONS, 1), pl.ds(0, 48)]),
        (owner_hbm, two.at[0]),
        (within_hbm, two.at[1]),
        (ids_hbm, two.at[2]),
    ]
    copies = [
        pltpu.make_async_copy(src, dst, local_sems.at[n]) for n, (src, dst) in enumerate(copies)
    ]
    for copy in copies:
        copy.start()

    barrier = pltpu.get_barrier_semaphore()
    neighbours = [*z_by.values(), *u_by.values(), *v_by.values(), peer]
    for device in neighbours:
        pl.semaphore_signal(barrier, inc=1, device_id=device, device_id_type=pl.DeviceIdType.MESH)

    links = Links(send_sems, recv_sems, peer)

    def piece(z_low_at, u_at, high=None):
        high = slice(None) if high is None else high
        return weights.at[:, high, z_low_at, v, :, own_columns(u_at)]

    def stripe(z_low_at, v_at, high=None):
        high = slice(None) if high is None else high
        return weights.at[
            :, high, z_low_at, v_at, :, pl.ds(pl.multiple_of(core * HALF, HALF), HALF)
        ]

    def column_half(z_low_at, which):
        return weights.at[:, :, z_low_at, :, :, pl.ds(pl.multiple_of(which * HALF, HALF), HALF)]

    first_half, last_half = pl.ds(0, SIDE // 2), pl.ds(SIDE // 2, SIDE // 2)
    sent = {}

    def z_far():
        copies[chunks].wait()
        for d in (4, -4, 8):
            sent["z", d] = links.send(piece(z_low, u, z_high), z_by[d])

    def z_near():
        for d in (4, -4, 8):
            links.arrive(sent["z", d], piece(z_low, u, along(-d) // SIDE))
        for d in (1, -1):
            sent["z", d] = links.send(piece(z_low, u), z_by[d])
        sent["z", 2] = links.send(piece(z_low, u, first_half), z_by[2])
        sent["z", -2] = links.send(piece(z_low, u, last_half), z_by[-2])

    def z_arrive(c):
        if c == 2:
            links.arrive(sent["z", 2], piece(turn(z_low, 2), u, first_half))
            links.arrive(sent["z", -2], piece(turn(z_low, 2), u, last_half))
        elif c:
            links.arrive(sent["z", -c], piece(turn(z_low, c), u))

    def u_step(c):
        z_arrive(c)
        for d in (1, -1):
            sent["u", c, d] = links.send(piece(turn(z_low, c), u), u_by[d])

    def u_far(c):
        at = turn(z_low, c)
        for d in (1, -1):
            links.arrive(sent["u", c, d], piece(at, turn(u, -d)))
        sent["u", c, 2] = links.send(piece(at, turn(u, -1), first_half), u_by[1])
        sent["u", c, -2] = links.send(piece(at, turn(u, 1), last_half), u_by[-1])

    def v_step(c):
        at = turn(z_low, c)
        links.arrive(sent["u", c, 2], piece(at, turn(u, 2), first_half))
        links.arrive(sent["u", c, -2], piece(at, turn(u, 2), last_half))
        for d in (1, -1):
            sent["v", c, d] = links.send(stripe(at, v), v_by[d])

    def v_far(c):
        at = turn(z_low, c)
        for d in (1, -1):
            links.arrive(sent["v", c, d], stripe(at, turn(v, -d)))
        sent["v", c, 2] = links.send(stripe(at, turn(v, -1), first_half), v_by[1])
        sent["v", c, -2] = links.send(stripe(at, turn(v, 1), last_half), v_by[-1])

    def across_step(c):
        at = turn(z_low, c)
        links.arrive(sent["v", c, 2], stripe(at, turn(v, 2), first_half))
        links.arrive(sent["v", c, -2], stripe(at, turn(v, 2), last_half))
        sent["across", c] = links.send(column_half(at, core), peer)

    plan = {
        2: [(z_near,), (u_step, 0)],
        4: [(u_far, 0), (u_step, 1), (u_step, -1)],
        6: [(u_step, 2), (v_step, 0), (u_far, 1), (u_far, -1)],
        8: [(v_step, 1), (v_step, -1), (u_far, 2)],
        9: [(v_far, 0)],
        10: [(v_step, 2)],
        12: [(across_step, 0), (v_far, 1)],
        14: [(v_far, -1), (across_step, 1)],
        16: [(v_far, 2), (across_step, -1)],
    }

    def serve(slot):
        for action, *given in plan.get(slot, ()):
            action(*given)

    for n in range(chunks):
        copies[n].wait()
        build_table(feats, table, n * span // LANES, (n + 1) * span // LANES)
        if n == 1:
            pl.semaphore_wait(barrier, len(neighbours))
            z_far()
    for copy in copies[chunks + 1 :]:
        copy.wait()
    build_relations(rel, by_row)
    w_one[:, 48:64, :] = jnp.zeros((6, 16, WIDTH), BF16)
    w_one[RELATIONS + 1, 0:48, :] = jnp.zeros((48, WIDTH), BF16)

    in_right, in_left = {}, {}
    steps = FEAT // 2
    quarter = WIDTH // 4
    for s in range(steps + 1):
        gather_block(along(steps - s), 0, nbr, table, by_row, picked, slabs)
        serve(2 * s)
        if 0 < s < steps:
            gather_block(along(s - steps), ROWS, nbr, table, by_row, picked, slabs)
        serve(2 * s + 1)
        rows = 2 * ROWS if 0 < s < steps else ROWS
        for h in range(4):
            columns = slice(h * quarter, (h + 1) * quarter)
            partial = jnp.dot(
                slabs[0:rows, :],
                w_one[:, :, columns].reshape(6 * 64, quarter),
                preferred_element_type=F32,
            )
            if s == 0:
                if h < 2:
                    send_right[0, h] = partial.astype(BF16)
                    in_right[0, h] = links.send(send_right.at[0, h], right, from_left.at[0, h])
                else:
                    send_left[0, h] = partial.astype(BF16)
                    in_left[0, h] = links.send(send_left.at[0, h], left, from_right.at[0, h])
                continue
            if s == steps:
                links.arrive(in_right[s - 1, h], from_left.at[s - 1, h])
                links.arrive(in_left[s - 1, h], from_right.at[s - 1, h])
                total = partial + from_left[s - 1, h].astype(F32) + from_right[s - 1, h].astype(F32)
                hidden[core, v, u, :, columns] = jnp.maximum(total, 0.0).astype(BF16)
                continue
            onward, back = partial[:ROWS], partial[ROWS:]
            if (s - 1, h) in in_right:
                links.arrive(in_right[s - 1, h], from_left.at[s - 1, h])
                onward = onward + from_left[s - 1, h].astype(F32)
            send_right[s, h] = onward.astype(BF16)
            in_right[s, h] = links.send(send_right.at[s, h], right, from_left.at[s, h])
            if (s - 1, h) in in_left:
                links.arrive(in_left[s - 1, h], from_right.at[s - 1, h])
                back = back + from_right[s - 1, h].astype(F32)
            send_left[s, h] = back.astype(BF16)
            in_left[s, h] = links.send(send_left.at[s, h], left, from_right.at[s, h])

    def rows_of(du, dv):
        return hidden.at[core, turn(v, dv), turn(u, du)]

    def rows_of_peer(du, dv):
        return hidden.at[1 - core, turn(u, dv), turn(v, du)]

    order = (0, -1, 1, 2)
    crossed = {}

    def cross(du, dv):
        crossed[du, dv] = links.send(rows_of(du, dv), peer)

    def to_v(du):
        for d in (1, -1, 2):
            sent["h", du, d] = links.send(rows_of(du, 0), v_by[d])

    def from_v(du, dv):
        links.arrive(sent["h", du, -dv if dv != 2 else 2], rows_of(du, dv))
        cross(du, dv)

    def add_group(which, v_at, first=False):
        group = which * SIDE + v_at
        columns = pl.ds(pl.multiple_of(group * 2 * LANES, 2 * LANES), 2 * LANES)

        def step(n, carry):
            at = pl.ds(pl.multiple_of(n * 256, 256), 256)
            rows = hidden[which, v_at, :, :, at].reshape(SIDE * ROWS, 256)
            product = jnp.dot(counts[:, columns], rows, preferred_element_type=F32)
            summed[:, at] = product if first else summed[:, at] + product
            return carry

        lax.fori_loop(0, WIDTH // 256, step, 0)

    def times_weights(slab, left_rows, first=False):
        def step(n, carry):
            at = pl.ds(pl.multiple_of(n * 256, 256), 256)
            w = weights[slab, :, :, :, :, at].reshape(WIDTH, 256)
            product = jnp.dot(left_rows, w, preferred_element_type=F32)
            result[:, at] = product if first else result[:, at] + product
            return carry

        lax.fori_loop(0, WIDTH // 256, step, 0)

    for d in (1, -1, 2):
        sent["hu", d] = links.send(rows_of(0, 0), u_by[d])
    to_v(0)
    cross(0, 0)

    block_row = z // 2
    owner, within, ids = (
        as_columns(two[n, :, pl.ds(block_row, 1), :].reshape(FANOUT_TWO, LANES)) for n in range(3)
    )
    owner = owner.astype(jnp.int32)
    parity, across_x, across_y = owner % 2, (owner // 2) % SIDE, owner // (2 * SIDE)
    held = across_y * SIDE + across_x + parity * (
        SIDE * SIDE + (SIDE - 1) * across_x - (SIDE - 1) * across_y
    )
    keys[...] = ids * float(BATCHES * ROWS) + held.astype(F32) * float(ROWS) + within
    ids_two[...] = ids
    mine = pl.ds(pl.multiple_of(lax.rem(z, 2) * ROWS, ROWS), ROWS)
    build_counts(keys.at[mine], counts)

    for du in (-1, 1, 2):
        links.arrive(sent["hu", -du if du != 2 else 2], rows_of(du, 0))
        to_v(du)
        cross(du, 0)
    add_group(core, v, first=True)
    for dv in (-1, 1, 2):
        from_v(0, dv)
    across_step(2)
    for c in (0, 1, -1, 2):
        links.arrive(sent["across", c], column_half(turn(z_low, c), 1 - core))
    times_weights(0, hidden[core, v, u], first=True)
    for du in order:
        links.arrive(crossed[du, 0], rows_of_peer(du, 0))
    add_group(1 - core, u)
    for dv in (-1, 1, 2):
        for du in (-1, 1, 2):
            from_v(du, dv)
        add_group(core, turn(v, dv))
    for dv in (-1, 1, 2):
        for du in order:
            links.arrive(crossed[du, dv], rows_of_peer(du, dv))
        add_group(1 - core, turn(u, dv))

    ids = ids_two[mine, :]
    for r in range(RELATIONS):
        number = jnp.sum(jnp.where(ids == float(r), 1.0, 0.0), axis=1, keepdims=True)
        mean = summed[r * ROWS : (r + 1) * ROWS, :] / jnp.maximum(number, 1.0)
        times_weights(r + 1, mean.astype(BF16))
    out[...] = jnp.maximum(result[...], 0.0).astype(BF16)
    links.finish()


COPIES = 144


def two_layers(nbr, feats, rel, w_one, owner, within, ids, w_two):
    sources = feats.shape[1]
    dest = WIDTH
    half_steps = FEAT // 2
    travelling = pltpu.VMEM((half_steps, 4, ROWS, WIDTH // 4), BF16)
    return pl.pallas_call(
        kernel,
        out_shape=jax.ShapeDtypeStruct((ROWS, WIDTH), BF16),
        in_specs=[pl.BlockSpec(memory_space=pl.ANY)] * 8,
        out_specs=pl.BlockSpec(memory_space=pltpu.VMEM),
        scratch_shapes=[
            pltpu.SMEM(nbr.shape, jnp.int32),
            pltpu.VMEM(feats.shape, BF16),
            pltpu.VMEM(rel.shape, jnp.int32),
            pltpu.VMEM((RELATIONS + 2, 64, WIDTH), BF16),
            pltpu.VMEM((3, *ids.shape), jnp.int32),
            pltpu.VMEM((sources, LANES), F32),
            pltpu.VMEM((dest, 16), F32),
            pltpu.VMEM((2, FANOUT_ONE * 8, LANES), F32),
            pltpu.VMEM((2 * ROWS, 3 * LANES), BF16),
            pltpu.VMEM((LANES, 16), F32),
            pltpu.VMEM((LANES, 16), F32),
            pltpu.VMEM((RELATIONS * ROWS, BATCHES * ROWS), BF16),
            pltpu.VMEM((RELATIONS + 1, SIDE, SIDE, SIDE, ROWS // SIDE, WIDTH), BF16),
            pltpu.VMEM((2, SIDE, SIDE, ROWS, WIDTH), BF16),
            travelling,
            travelling,
            travelling,
            travelling,
            pltpu.VMEM((RELATIONS * ROWS, WIDTH), F32),
            pltpu.VMEM((ROWS, WIDTH), F32),
            pltpu.SemaphoreType.DMA((COPIES,)),
            pltpu.SemaphoreType.DMA((COPIES,)),
            pltpu.SemaphoreType.DMA((12,)),
        ],
        compiler_params=pltpu.CompilerParams(
            vmem_limit_bytes=48 << 20, collective_id=0, has_side_effects=True
        ),
        cost_estimate=pl.CostEstimate(
            flops=2_400_000_000, bytes_accessed=4_000_000, transcendentals=0
        ),
        name="two_layers",
    )(nbr, feats, rel, w_one, owner, within, ids, w_two)


def body(feats, nbr_one, rel_one, w_one, owner_two, local_two, rel_two, w_two):
    def slots_first(array):
        return array.T.reshape(FANOUT_TWO, DEST_ROWS, LANES)

    out = two_layers(
        nbr_one[0].reshape(FANOUT_ONE, DEST_ROWS, LANES),
        feats[0],
        rel_one[0].reshape(FANOUT_ONE, DEST_ROWS, LANES),
        w_one,
        slots_first(owner_two[0, :, :, 0]),
        slots_first(local_two[0]),
        slots_first(rel_two[0]),
        w_two.reshape(RELATIONS + 1, SIDE, ROWS // SIDE, WIDTH),
    )
    return out[None]


def solution(mesh):
    in_specs = (
        P("batch", "feat", None),
        P("batch", None, None),
        P("batch", None, None),
        P(None, "feat", None),
        P("batch", None, None, None),
        P("batch", None, None),
        P("batch", None, None),
        P(None, "feat", None),
    )
    out_specs = P("batch", "feat", None)
    return jax.shard_map(body, mesh=mesh, in_specs=in_specs, out_specs=out_specs, check_vma=False)
```

time: 123 us -> 98.9 us (0.80)
  Pallas kernels: 115 us -> 92.4 us
  other arithmetic: 3.36 us -> 0 us
  local copies, waits for them, and re-layouts: 4.36 us -> 6.1 us
    pallas_call x1, Pallas kernels: 115 us -> 92.4 us  [two_layers(): pl.pallas_call(kernel, out_shape=jax.ShapeDtypeStruct((ROWS, WIDTH), BF16...]
    unnamed x10 -> x17, local copies, waits for them, and re-layouts: 2.26 us -> 6.08 us
    add x2 -> x0, other arithmetic: 2.33 us -> none  [the longest x1 2.3 us: count_table(): table = table + (keys[:, slot][:, None] == labels[None, :]).astype(BF16)]
where the time goes in v3:
time: 98.9 us; the launch traced here: 98.6 us
  Pallas kernels  92.4 us (93%)
  local copies, waits for them, and re-layouts  6.1 us (6%)
    pallas_call x1, Pallas kernels, two_layers(): pl.pallas_call(kernel, out_shape=jax.ShapeDtypeStruct((ROWS, WIDTH), BF16...  92.4 us
    unnamed x17, local copies, waits for them, and re-layouts  6.08 us

profile of v3, /device:TPU:1, one launch (start us, length us, event | category | flops | bytes accessed | tf_op | source)
XLA Modules:
  0.0 98.6 jit_solution(11032213309172897194)
XLA Ops:
  0.0 0.0 copy-start
  0.0 0.9 copy.9
  0.9 0.8 copy.10
  1.7 0.8 copy.11
  2.5 0.0 copy-start.4
  2.6 0.0 copy-start.3
  2.6 0.0 copy-done
  2.6 0.8 copy-done.4
  3.4 0.0 copy-done.3
  3.4 0.0 copy-start.1
  3.4 1.1 %copy-done.1 = bf16[5,64,1024]{2,1,0:T(8,128)(2,1)S(1)} copy-done((bf16[5,64,1024]{2,1,0:T(8,128)(2,1)S(1)}, bf16[5,64,1024]{2,1,0:T(8,128)(2,1)}, u32[]{:S(2)}) %copy-start.1) | copy-done | bytes 655384
  4.5 0.0 copy-start.2
  4.5 1.0 %copy-done.2 = bf16[5,48,1024]{2,1,0:T(8,128)(2,1)S(1)} copy-done((bf16[5,48,1024]{2,1,0:T(8,128)(2,1)S(1)}, bf16[5,48,1024]{2,1,0:T(8,128)(2,1)}, u32[]{:S(2)}) %copy-start.2) | copy-done | bytes 491544
  5.5 92.4 %two_layers.1 = bf16[64,1024]{1,0:T(8,128)(2,1)S(1)} custom-call(s32[15,8,128]{2,1,0:T(8,128)S(1)} %bitcast.26, bf16[48,8192]{1,0:T(8,128)(2,1)S(1)} %bitcast.24, s32[15,8,128]{2,1,0:T(8,128)S(1)} %bitcast.27, bf16[5,48,1024]{2,1,0:T(8,128)(2,1)S(1)} %copy-done.2, s32[10,8,128]{2,1,0:T(8,128)S(1)} %slice.owner_hbm, s32[10,8,128]{2,1,0:T(8,128)S(1)} %slice.1.within_hbm, ...), custom_call_target="tpu_custom_call" | custom-call | flops 2400000000 | bytes 4000000 | tf_op jit(solution)/shard_map/two_layers/pallas_call | solution.py:470
  97.9 0.7 copy.16
  (6 shorter events, 0.1 us)
Async XLA Ops:
  0.0 2.6 %copy-start = (bf16[1,48,8192]{2,1,0:T(8,128)(2,1)S(1)}, bf16[1,48,8192]{2,1,0:T(8,128)(2,1)}, u32[]{:S(2)}) copy-start(bf16[1,48,8192]{2,1,0:T(8,128)(2,1)} %param.8) | copy-start | bytes 2359300
  2.5 0.8 copy-start.4
  2.6 0.8 copy-start.3
  3.4 1.1 %copy-start.1 = (bf16[5,64,1024]{2,1,0:T(8,128)(2,1)S(1)}, bf16[5,64,1024]{2,1,0:T(8,128)(2,1)}, u32[]{:S(2)}) copy-start(bf16[5,64,1024]{2,1,0:T(8,128)(2,1)} %param.15) | copy-start | bytes 1966084
  4.5 1.0 %copy-start.2 = (bf16[5,48,1024]{2,1,0:T(8,128)(2,1)S(1)}, bf16[5,48,1024]{2,1,0:T(8,128)(2,1)}, u32[]{:S(2)}) copy-start(bf16[5,48,1024]{2,1,0:T(8,128)(2,1)} %w_one_hbm.1) | copy-start | bytes 1474564

commit v4 on v3

--- a/solution.py
+++ b/solution.py
@@ -116,22 +116,31 @@
     slabs[to : to + ROWS, 2 * LANES :] = table[pl.ds(first, ROWS), :].astype(BF16)
 
 
-def build_counts(keys, counts):
+def build_counts(keys, counts, first_row):
     span = counts.shape[1]
 
     def some_rows(n, carry):
         at = pl.multiple_of(n * 16, 16)
         key = keys[pl.ds(at, 16), :]
-        spread = [jnp.broadcast_to(key[:, k : k + 1], (16, LANES)) for k in range(FANOUT_TWO)]
+        tiles = jnp.floor(key * (1.0 / LANES))
         lane = lax.broadcasted_iota(jnp.int32, (16, LANES), 1).astype(F32)
+        tile_of, ones = [], []
+        for k in range(FANOUT_TWO):
+            column = jnp.broadcast_to(key[:, k : k + 1], (16, LANES))
+            tile = jnp.broadcast_to(tiles[:, k : k + 1], (16, LANES))
+            tile_of.append(tile.astype(BF16))
+            ones.append(jnp.where(column - tile * LANES == lane, 1.0, 0.0).astype(BF16))
+        zero = jnp.zeros((16, LANES), BF16)
         for r in range(RELATIONS):
             for c in range(span // LANES):
-                label = lane + float(r * span + c * LANES)
-                total = jnp.zeros((16, LANES), F32)
-                for k in range(FANOUT_TWO):
-                    total = total + jnp.where(spread[k] == label, 1.0, 0.0)
-                rows = pl.ds(r * ROWS + at, 16)
-                counts[rows, c * LANES : (c + 1) * LANES] = total.astype(BF16)
+                label = jnp.full((16, LANES), r * (span // LANES) + c, BF16)
+                parts = [
+                    jnp.where(tile_of[k] == label, ones[k], zero) for k in range(FANOUT_TWO)
+                ]
+                while len(parts) > 1:
+                    parts = [sum(parts[i : i + 2][1:], parts[i]) for i in range(0, len(parts), 2)]
+                rows = pl.ds(r * SIDE * ROWS + first_row + at, 16)
+                counts[rows, c * LANES : (c + 1) * LANES] = parts[0]
         return carry
 
     lax.fori_loop(0, ROWS // 16, some_rows, 0)
@@ -156,8 +165,8 @@
     by_row,
     picked,
     slabs,
+    columns_two,
     keys,
-    ids_two,
     counts,
     weights,
     hidden,
@@ -166,7 +175,9 @@
     from_left,
     from_right,
     summed,
-    result,
+    left_rows,
+    finished,
+    arrived,
     send_sems,
     recv_sems,
     local_sems,
@@ -192,11 +203,17 @@
     z_by = {d: (along(d), place) for d in (1, -1, 2, -2, 4, -4, 8)}
     u_by = {d: in_plane(turn(u, d), v) for d in (1, -1, 2)}
     v_by = {d: in_plane(u, turn(v, d)) for d in (1, -1, 2)}
+    x_by = {d: (z, y * 2 * SIDE + turn(x, d) * 2 + core) for d in (1, -1, 2)}
+    y_by = {d: (z, turn(y, d) * 2 * SIDE + x * 2 + core) for d in (1, -1, 2)}
     right, left = z_by[1], z_by[-1]
     peer = (z, place + 1 - 2 * core)
 
-    def own_columns(u_at):
-        return pl.ds(pl.multiple_of((core * SIDE + u_at) * LANES, LANES), LANES)
+    wide = WIDTH // SIDE
+
+    def lanes_of(which):
+        return pl.ds(pl.multiple_of(which * LANES, LANES), LANES)
+
+    here = pl.ds(pl.multiple_of(x * wide + core * LANES, LANES), LANES)
 
     chunks = 4
     span = feats.shape[1] // chunks
@@ -204,7 +221,7 @@
         (feats_hbm.at[:, pl.ds(n * span, span)], feats.at[:, pl.ds(n * span, span)])
         for n in range(chunks)
     ] + [
-        (w_two.at[:, v, :, own_columns(u)], weights.at[:, z_high, z_low, v, :, own_columns(u)]),
+        (w_two.at[:, y, :, here], weights.at[:, z_high, z_low, y, :, lanes_of(core)]),
         (nbr_hbm, nbr),
         (rel_hbm, rel),
         (w_one_hbm.at[pl.ds(1, RELATIONS)], w_one.at[pl.ds(0, RELATIONS), pl.ds(0, 48)]),
@@ -226,18 +243,12 @@
 
     links = Links(send_sems, recv_sems, peer)
 
-    def piece(z_low_at, u_at, high=None):
+    def piece(z_low_at, y_at, high=None):
         high = slice(None) if high is None else high
-        return weights.at[:, high, z_low_at, v, :, own_columns(u_at)]
-
-    def stripe(z_low_at, v_at, high=None):
-        high = slice(None) if high is None else high
-        return weights.at[
-            :, high, z_low_at, v_at, :, pl.ds(pl.multiple_of(core * HALF, HALF), HALF)
-        ]
+        return weights.at[:, high, z_low_at, y_at, :, lanes_of(core)]
 
     def column_half(z_low_at, which):
-        return weights.at[:, :, z_low_at, :, :, pl.ds(pl.multiple_of(which * HALF, HALF), HALF)]
+        return weights.at[:, :, z_low_at, :, :, lanes_of(which)]
 
     first_half, last_half = pl.ds(0, SIDE // 2), pl.ds(SIDE // 2, SIDE // 2)
     sent = {}
@@ -245,65 +256,52 @@
     def z_far():
         copies[chunks].wait()
         for d in (4, -4, 8):
-            sent["z", d] = links.send(piece(z_low, u, z_high), z_by[d])
+            sent["z", d] = links.send(piece(z_low, y, z_high), z_by[d])
 
     def z_near():
         for d in (4, -4, 8):
-            links.arrive(sent["z", d], piece(z_low, u, along(-d) // SIDE))
+            links.arrive(sent["z", d], piece(z_low, y, along(-d) // SIDE))
         for d in (1, -1):
-            sent["z", d] = links.send(piece(z_low, u), z_by[d])
-        sent["z", 2] = links.send(piece(z_low, u, first_half), z_by[2])
-        sent["z", -2] = links.send(piece(z_low, u, last_half), z_by[-2])
+            sent["z", d] = links.send(piece(z_low, y), z_by[d])
+        sent["z", 2] = links.send(piece(z_low, y, first_half), z_by[2])
+        sent["z", -2] = links.send(piece(z_low, y, last_half), z_by[-2])
 
     def z_arrive(c):
         if c == 2:
-            links.arrive(sent["z", 2], piece(turn(z_low, 2), u, first_half))
-            links.arrive(sent["z", -2], piece(turn(z_low, 2), u, last_half))
+            links.arrive(sent["z", 2], piece(turn(z_low, 2), y, first_half))
+            links.arrive(sent["z", -2], piece(turn(z_low, 2), y, last_half))
         elif c:
-            links.arrive(sent["z", -c], piece(turn(z_low, c), u))
-
-    def u_step(c):
+            links.arrive(sent["z", -c], piece(turn(z_low, c), y))
+
+    def y_step(c):
         z_arrive(c)
         for d in (1, -1):
-            sent["u", c, d] = links.send(piece(turn(z_low, c), u), u_by[d])
-
-    def u_far(c):
+            sent["y", c, d] = links.send(piece(turn(z_low, c), y), y_by[d])
+
+    def y_far(c):
         at = turn(z_low, c)
         for d in (1, -1):
-            links.arrive(sent["u", c, d], piece(at, turn(u, -d)))
-        sent["u", c, 2] = links.send(piece(at, turn(u, -1), first_half), u_by[1])
-        sent["u", c, -2] = links.send(piece(at, turn(u, 1), last_half), u_by[-1])
-
-    def v_step(c):
-        at = turn(z_low, c)
-        links.arrive(sent["u", c, 2], piece(at, turn(u, 2), first_half))
-        links.arrive(sent["u", c, -2], piece(at, turn(u, 2), last_half))
-        for d in (1, -1):
-            sent["v", c, d] = links.send(stripe(at, v), v_by[d])
-
-    def v_far(c):
-        at = turn(z_low, c)
-        for d in (1, -1):
-            links.arrive(sent["v", c, d], stripe(at, turn(v, -d)))
-        sent["v", c, 2] = links.send(stripe(at, turn(v, -1), first_half), v_by[1])
-        sent["v", c, -2] = links.send(stripe(at, turn(v, 1), last_half), v_by[-1])
+            links.arrive(sent["y", c, d], piece(at, turn(y, -d)))
+        sent["y", c, 2] = links.send(piece(at, turn(y, -1), first_half), y_by[1])
+        sent["y", c, -2] = links.send(piece(at, turn(y, 1), last_half), y_by[-1])
 
     def across_step(c):
         at = turn(z_low, c)
-        links.arrive(sent["v", c, 2], stripe(at, turn(v, 2), first_half))
-        links.arrive(sent["v", c, -2], stripe(at, turn(v, 2), last_half))
+        links.arrive(sent["y", c, 2], piece(at, turn(y, 2), first_half))
+        links.arrive(sent["y", c, -2], piece(at, turn(y, 2), last_half))
         sent["across", c] = links.send(column_half(at, core), peer)
 
     plan = {
-        2: [(z_near,), (u_step, 0)],
-        4: [(u_far, 0), (u_step, 1), (u_step, -1)],
-        6: [(u_step, 2), (v_step, 0), (u_far, 1), (u_far, -1)],
-        8: [(v_step, 1), (v_step, -1), (u_far, 2)],
-        9: [(v_far, 0)],
-        10: [(v_step, 2)],
-        12: [(across_step, 0), (v_far, 1)],
-        14: [(v_far, -1), (across_step, 1)],
-        16: [(v_far, 2), (across_step, -1)],
+        3: [(z_near,), (y_step, 0)],
+        6: [(y_far, 0)],
+        7: [(y_step, 1), (y_step, -1)],
+        8: [(y_step, 2)],
+        10: [(across_step, 0), (y_far, 1)],
+        11: [(y_far, -1)],
+        12: [(y_far, 2)],
+        14: [(across_step, 1)],
+        15: [(across_step, -1)],
+        16: [(across_step, 2)],
     }
 
     def serve(slot):
@@ -319,6 +317,21 @@
     for copy in copies[chunks + 1 :]:
         copy.wait()
     build_relations(rel, by_row)
+    block_row = z // 2
+    owner, within, ids = (
+        as_columns(two[n, :, pl.ds(block_row, 1), :].reshape(FANOUT_TWO, LANES)) for n in range(3)
+    )
+    owner = owner.astype(jnp.int32)
+    parity, across_x, across_y = owner % 2, (owner // 2) % SIDE, owner // (2 * SIDE)
+    held = across_y * SIDE + across_x + parity * (
+        SIDE * SIDE + (SIDE - 1) * across_x - (SIDE - 1) * across_y
+    )
+    columns_two[...] = ids * float(BATCHES * ROWS) + held.astype(F32) * float(ROWS) + within
+    mine = pl.ds(pl.multiple_of(lax.rem(z, 2) * ROWS, ROWS), ROWS)
+    none = jnp.full((ROWS, LANES - 16), float(RELATIONS * BATCHES * ROWS), F32)
+    keys[x] = jnp.concatenate([columns_two[mine, :], none], axis=1)
+    for d in (1, -1, 2):
+        sent["keys", d] = links.send(keys.at[x], x_by[d])
     w_one[:, 48:64, :] = jnp.zeros((6, 16, WIDTH), BF16)
     w_one[RELATIONS + 1, 0:48, :] = jnp.zeros((48, WIDTH), BF16)
 
@@ -378,12 +391,28 @@
         crossed[du, dv] = links.send(rows_of(du, dv), peer)
 
     def to_v(du):
-        for d in (1, -1, 2):
+        for d in (1, -1, 2) if du == 2 else (1, -1):
             sent["h", du, d] = links.send(rows_of(du, 0), v_by[d])
 
-    def from_v(du, dv):
-        links.arrive(sent["h", du, -dv if dv != 2 else 2], rows_of(du, dv))
-        cross(du, dv)
+    def half_of(ref, which):
+        return ref.at[pl.ds(which * (ROWS // 2), ROWS // 2)]
+
+    def from_v(du):
+        for d in (1, -1):
+            links.arrive(sent["h", du, d], rows_of(du, -d))
+        if du != 2:
+            sent["h", du, 2] = links.send(half_of(rows_of(du, -1), 0), v_by[1])
+            sent["h", du, -2] = links.send(half_of(rows_of(du, 1), 1), v_by[-1])
+        cross(du, -1)
+        cross(du, 1)
+
+    def from_v_far(du):
+        if du == 2:
+            links.arrive(sent["h", du, 2], rows_of(du, 2))
+        else:
+            links.arrive(sent["h", du, 2], half_of(rows_of(du, 2), 0))
+            links.arrive(sent["h", du, -2], half_of(rows_of(du, 2), 1))
+        cross(du, 2)
 
     def add_group(which, v_at, first=False):
         group = which * SIDE + v_at
@@ -392,18 +421,10 @@
         def step(n, carry):
             at = pl.ds(pl.multiple_of(n * 256, 256), 256)
             rows = hidden[which, v_at, :, :, at].reshape(SIDE * ROWS, 256)
-            product = jnp.dot(counts[:, columns], rows, preferred_element_type=F32)
-            summed[:, at] = product if first else summed[:, at] + product
-            return carry
-
-        lax.fori_loop(0, WIDTH // 256, step, 0)
-
-    def times_weights(slab, left_rows, first=False):
-        def step(n, carry):
-            at = pl.ds(pl.multiple_of(n * 256, 256), 256)
-            w = weights[slab, :, :, :, :, at].reshape(WIDTH, 256)
-            product = jnp.dot(left_rows, w, preferred_element_type=F32)
-            result[:, at] = product if first else result[:, at] + product
+            for r in range(RELATIONS):
+                some = slice(r * SIDE * ROWS, (r + 1) * SIDE * ROWS)
+                product = jnp.dot(counts[some, columns], rows, preferred_element_type=F32)
+                summed[some, at] = product if first else summed[some, at] + product
             return carry
 
         lax.fori_loop(0, WIDTH // 256, step, 0)
@@ -413,49 +434,64 @@
     to_v(0)
     cross(0, 0)
 
-    block_row = z // 2
-    owner, within, ids = (
-        as_columns(two[n, :, pl.ds(block_row, 1), :].reshape(FANOUT_TWO, LANES)) for n in range(3)
-    )
-    owner = owner.astype(jnp.int32)
-    parity, across_x, across_y = owner % 2, (owner // 2) % SIDE, owner // (2 * SIDE)
-    held = across_y * SIDE + across_x + parity * (
-        SIDE * SIDE + (SIDE - 1) * across_x - (SIDE - 1) * across_y
-    )
-    keys[...] = ids * float(BATCHES * ROWS) + held.astype(F32) * float(ROWS) + within
-    ids_two[...] = ids
-    mine = pl.ds(pl.multiple_of(lax.rem(z, 2) * ROWS, ROWS), ROWS)
-    build_counts(keys.at[mine], counts)
-
+    def count(d):
+        if d:
+            links.arrive(sent["keys", d], keys.at[turn(x, -d)])
+        build_counts(keys.at[turn(x, -d)], counts, turn(x, -d) * ROWS)
+
+    count(0)
+    count(1)
     for du in (-1, 1, 2):
         links.arrive(sent["hu", -du if du != 2 else 2], rows_of(du, 0))
         to_v(du)
         cross(du, 0)
+    count(-1)
+    from_v(0)
+    count(2)
     add_group(core, v, first=True)
-    for dv in (-1, 1, 2):
-        from_v(0, dv)
-    across_step(2)
-    for c in (0, 1, -1, 2):
-        links.arrive(sent["across", c], column_half(turn(z_low, c), 1 - core))
-    times_weights(0, hidden[core, v, u], first=True)
+    for du in (-1, 1):
+        from_v(du)
     for du in order:
         links.arrive(crossed[du, 0], rows_of_peer(du, 0))
     add_group(1 - core, u)
-    for dv in (-1, 1, 2):
-        for du in (-1, 1, 2):
-            from_v(du, dv)
-        add_group(core, turn(v, dv))
+    from_v_far(0)
+    from_v(2)
+    add_group(core, turn(v, -1))
+    from_v_far(2)
+    from_v_far(-1)
+    from_v_far(1)
+    add_group(core, turn(v, 1))
+    add_group(core, turn(v, 2))
     for dv in (-1, 1, 2):
         for du in order:
             links.arrive(crossed[du, dv], rows_of_peer(du, dv))
         add_group(1 - core, turn(u, dv))
-
-    ids = ids_two[mine, :]
-    for r in range(RELATIONS):
-        number = jnp.sum(jnp.where(ids == float(r), 1.0, 0.0), axis=1, keepdims=True)
-        mean = summed[r * ROWS : (r + 1) * ROWS, :] / jnp.maximum(number, 1.0)
-        times_weights(r + 1, mean.astype(BF16))
-    out[...] = jnp.maximum(result[...], 0.0).astype(BF16)
+    for c in (0, 1, -1, 2):
+        links.arrive(sent["across", c], column_half(turn(z_low, c), 1 - core))
+
+    ring_rows = SIDE * ROWS
+    for n in range(SIDE):
+        own = hidden[core, y + core * (n - y), n + core * (y - n)]
+        left_rows[0, n * ROWS : (n + 1) * ROWS, :] = own
+        key = keys[n]
+        for r in range(RELATIONS):
+            low, high = float(r * BATCHES * ROWS), float((r + 1) * BATCHES * ROWS)
+            inside = jnp.where((key >= low) & (key < high), 1.0, 0.0)
+            number = jnp.maximum(jnp.sum(inside, axis=1, keepdims=True), 1.0)
+            some = slice(r * ring_rows + n * ROWS, r * ring_rows + (n + 1) * ROWS)
+            left_rows[r + 1, n * ROWS : (n + 1) * ROWS, :] = (summed[some, :] / number).astype(BF16)
+    total = jnp.zeros((ring_rows, wide), F32)
+    for slab in range(RELATIONS + 1):
+        w = weights[slab].reshape(WIDTH, wide)
+        total = total + jnp.dot(left_rows[slab], w, preferred_element_type=F32)
+    finished[...] = jnp.maximum(total, 0.0).astype(BF16).reshape(SIDE, ROWS, wide)
+    for d in (1, -1, 2):
+        sent["out", d] = links.send(finished.at[turn(x, d)], x_by[d], arrived.at[x])
+    arrived[x] = finished[x]
+    for d in (1, -1, 2):
+        links.arrive(sent["out", d], arrived.at[turn(x, -d)])
+    for n in range(SIDE):
+        out[:, n * wide : (n + 1) * wide] = arrived[n]
     links.finish()
 
 
@@ -483,22 +519,24 @@
             pltpu.VMEM((2, FANOUT_ONE * 8, LANES), F32),
             pltpu.VMEM((2 * ROWS, 3 * LANES), BF16),
             pltpu.VMEM((LANES, 16), F32),
-            pltpu.VMEM((LANES, 16), F32),
-            pltpu.VMEM((RELATIONS * ROWS, BATCHES * ROWS), BF16),
-            pltpu.VMEM((RELATIONS + 1, SIDE, SIDE, SIDE, ROWS // SIDE, WIDTH), BF16),
+            pltpu.VMEM((SIDE, ROWS, LANES), F32),
+            pltpu.VMEM((RELATIONS * SIDE * ROWS, BATCHES * ROWS), BF16),
+            pltpu.VMEM((RELATIONS + 1, SIDE, SIDE, SIDE, ROWS // SIDE, WIDTH // SIDE), BF16),
             pltpu.VMEM((2, SIDE, SIDE, ROWS, WIDTH), BF16),
             travelling,
             travelling,
             travelling,
             travelling,
-            pltpu.VMEM((RELATIONS * ROWS, WIDTH), F32),
-            pltpu.VMEM((ROWS, WIDTH), F32),
+            pltpu.VMEM((RELATIONS * SIDE * ROWS, WIDTH), F32),
+            pltpu.VMEM((RELATIONS + 1, SIDE * ROWS, WIDTH), BF16),
+            pltpu.VMEM((SIDE, ROWS, WIDTH // SIDE), BF16),
+            pltpu.VMEM((SIDE, ROWS, WIDTH // SIDE), BF16),
             pltpu.SemaphoreType.DMA((COPIES,)),
             pltpu.SemaphoreType.DMA((COPIES,)),
             pltpu.SemaphoreType.DMA((12,)),
         ],
         compiler_params=pltpu.CompilerParams(
-            vmem_limit_bytes=48 << 20, collective_id=0, has_side_effects=True
+            vmem_limit_bytes=62 << 20, collective_id=0, has_side_effects=True
         ),
         cost_estimate=pl.CostEstimate(
             flops=2_400_000_000, bytes_accessed=4_000_000, transcendentals=0
@@ -509,7 +547,7 @@
 
 def body(feats, nbr_one, rel_one, w_one, owner_two, local_two, rel_two, w_two):
     def slots_first(array):
-        return array.T.reshape(FANOUT_TWO, DEST_ROWS, LANES)
+        return array.reshape(DEST_ROWS, LANES, FANOUT_TWO).transpose(2, 0, 1)
 
     out = two_layers(
         nbr_one[0].reshape(FANOUT_ONE, DEST_ROWS, LANES),

time: 98.9 us -> 91.5 us (0.925)
  the two profiles are of different devices: /device:TPU:1 before, /device:TPU:4 now
where the time goes in v4:
time: 91.5 us; the launch traced here: 91.4 us
  Pallas kernels  89.8 us (98%)
  local copies, waits for them, and re-layouts  1.57 us (2%)
    pallas_call x1, Pallas kernels, two_layers(): pl.pallas_call(kernel, out_shape=jax.ShapeDtypeStruct((ROWS, WIDTH), BF16...  89.8 us

profile of v4, /device:TPU:4, one launch (start us, length us, event | category | flops | bytes accessed | tf_op | source)
XLA Modules:
  0.0 91.4 jit_solution(9835709033783549165)
XLA Ops:
  0.0 89.8 %two_layers.1 = bf16[64,1024]{1,0:T(8,128)(2,1)} custom-call(s32[15,8,128]{2,1,0:T(8,128)} %bitcast.17, bf16[48,8192]{1,0:T(8,128)(2,1)} %bitcast.15, s32[15,8,128]{2,1,0:T(8,128)} %bitcast.18, bf16[5,48,1024]{2,1,0:T(8,128)(2,1)} %w_one_hbm.1, s32[10,8,128]{2,1,0:T(8,128)} %bitcast.19, s32[10,8,128]{2,1,0:T(8,128)} %bitcast.20, s32[10,8,128]{2,1,0:T(8,128)} %bitcast.21, ...), custom_call_target="tpu_custom_call" | custom-call | flops 2400000000 | bytes 4000000 | tf_op jit(solution)/shard_map/two_layers/pallas_call | solution.py:506
  89.8 1.6 %copy.10 = bf16[1,64,1024]{2,1,0:T(8,128)(2,1)} copy(bf16[1,64,1024]{2,1,0:T(8,128)(2,1)} %bitcast.14) | data formatting | bytes 262144

commit v5 on v4

--- a/solution.py
+++ b/solution.py
@@ -54,10 +54,11 @@
 
 
 def build_table(feats, table, first, last):
+    gap = jnp.where(lax.broadcasted_iota(jnp.int32, (16, LANES), 0) == 15, 1.0, 0.0)
+
     def step(chunk, carry):
         at = pl.multiple_of(chunk * LANES, LANES)
         columns = feats[:, pl.ds(at, LANES)].astype(F32)
-        gap = jnp.zeros((LANES // 2 - columns.shape[0], LANES), F32)
         table[pl.ds(at, LANES), :] = jnp.concatenate([columns, gap, columns, gap], axis=0).T
         return carry
 
@@ -84,20 +85,25 @@
             source = nbr[k, row, column + i]
             picked[k * 8 + i : k * 8 + i + 1, :] = table[pl.ds(source, 1), :]
     zero = jnp.zeros(tile, F32)
-    low, high, low_count, high_count = zero, zero, zero, zero
+    low, high = zero, zero
     for k in range(FANOUT_ONE):
         rows = picked[k * 8 : (k + 1) * 8, :]
         own = jnp.broadcast_to(ids[:, k : k + 1], tile)
-        in_low, in_high = own == half, own == half + 2.0
-        low = low + jnp.where(in_low, rows, 0.0)
-        high = high + jnp.where(in_high, rows, 0.0)
-        low_count = low_count + jnp.where(in_low, 1.0, 0.0)
-        high_count = high_count + jnp.where(in_high, 1.0, 0.0)
-    return low / jnp.maximum(low_count, 1.0), high / jnp.maximum(high_count, 1.0)
+        low = low + jnp.where(own == half, rows, 0.0)
+        high = high + jnp.where(own == half + 2.0, rows, 0.0)
+
+    def mean(total):
+        first = jnp.broadcast_to(total[:, 63:64], tile)
+        second = jnp.broadcast_to(total[:, 127:128], tile)
+        return total / jnp.maximum(jnp.where(half == 0.0, first, second), 1.0)
+
+    return mean(low), mean(high)
 
 
 def gather_block(block, to, nbr, table, by_row, picked, slabs):
     row, start = block // 2, lax.rem(block, 2) * ROWS
+    lane = lax.broadcasted_iota(jnp.int32, (16, LANES), 1)
+    spare = lax.rem(lane, 64) >= 48
 
     def step(group, carry):
         at = pl.multiple_of(group * 16, 16)
@@ -106,14 +112,18 @@
             eight_means(base + n * 8, row, start + at + n * 8, nbr, table, by_row, picked.at[n])
             for n in range(2)
         ]
+        own = table[pl.ds(base, 16), :]
+        beside = (
+            jnp.where(lane < 64, pltpu.roll(own, 48, 1), pltpu.roll(own, 32, 1)),
+            pltpu.roll(own, 16, 1),
+        )
         for side in range(2):
             both = jnp.concatenate([pair[side] for pair in pairs], axis=0)
+            both = jnp.where(spare, beside[side], both)
             slabs[pl.ds(to + at, 16), side * LANES : (side + 1) * LANES] = both.astype(BF16)
         return carry
 
     lax.fori_loop(0, ROWS // 16, step, 0)
-    first = pl.multiple_of(block * ROWS, ROWS)
-    slabs[to : to + ROWS, 2 * LANES :] = table[pl.ds(first, ROWS), :].astype(BF16)
 
 
 def build_counts(keys, counts, first_row):
@@ -175,7 +185,9 @@
     from_left,
     from_right,
     summed,
+    inverse,
     left_rows,
+    accumulated,
     finished,
     arrived,
     send_sems,
@@ -224,8 +236,11 @@
         (w_two.at[:, y, :, here], weights.at[:, z_high, z_low, y, :, lanes_of(core)]),
         (nbr_hbm, nbr),
         (rel_hbm, rel),
-        (w_one_hbm.at[pl.ds(1, RELATIONS)], w_one.at[pl.ds(0, RELATIONS), pl.ds(0, 48)]),
-        (w_one_hbm.at[pl.ds(0, 1)], w_one.at[pl.ds(RELATIONS, 1), pl.ds(0, 48)]),
+        (w_one_hbm.at[pl.ds(1, RELATIONS)], w_one.at[:, pl.ds(0, 48)]),
+        *(
+            (w_one_hbm.at[pl.ds(0, 1), pl.ds(16 * n, 16)], w_one.at[pl.ds(n, 1), pl.ds(48, 16)])
+            for n in range(3)
+        ),
         (owner_hbm, two.at[0]),
         (within_hbm, two.at[1]),
         (ids_hbm, two.at[2]),
@@ -332,8 +347,20 @@
     keys[x] = jnp.concatenate([columns_two[mine, :], none], axis=1)
     for d in (1, -1, 2):
         sent["keys", d] = links.send(keys.at[x], x_by[d])
-    w_one[:, 48:64, :] = jnp.zeros((6, 16, WIDTH), BF16)
-    w_one[RELATIONS + 1, 0:48, :] = jnp.zeros((48, WIDTH), BF16)
+    w_one[3, 48:64, :] = jnp.zeros((16, WIDTH), BF16)
+
+    def count(d):
+        n = turn(x, -d)
+        if d:
+            links.arrive(sent["keys", d], keys.at[n])
+        build_counts(keys.at[n], counts, n * ROWS)
+        key = keys[n]
+        for r in range(RELATIONS):
+            low, high = float(r * BATCHES * ROWS), float((r + 1) * BATCHES * ROWS)
+            inside = jnp.where((key >= low) & (key < high), 1.0, 0.0)
+            number = jnp.maximum(jnp.sum(inside, axis=1, keepdims=True), 1.0)
+            some = pl.ds(pl.multiple_of(r * SIDE * ROWS + n * ROWS, ROWS), ROWS)
+            inverse[some, :] = jnp.broadcast_to(1.0 / number, (ROWS, LANES))
 
     in_right, in_left = {}, {}
     steps = FEAT // 2
@@ -344,12 +371,15 @@
         if 0 < s < steps:
             gather_block(along(s - steps), ROWS, nbr, table, by_row, picked, slabs)
         serve(2 * s + 1)
+        if s == steps:
+            count(0)
+            count(1)
         rows = 2 * ROWS if 0 < s < steps else ROWS
         for h in range(4):
             columns = slice(h * quarter, (h + 1) * quarter)
             partial = jnp.dot(
                 slabs[0:rows, :],
-                w_one[:, :, columns].reshape(6 * 64, quarter),
+                w_one[:, :, columns].reshape(RELATIONS * 64, quarter),
                 preferred_element_type=F32,
             )
             if s == 0:
@@ -434,13 +464,6 @@
     to_v(0)
     cross(0, 0)
 
-    def count(d):
-        if d:
-            links.arrive(sent["keys", d], keys.at[turn(x, -d)])
-        build_counts(keys.at[turn(x, -d)], counts, turn(x, -d) * ROWS)
-
-    count(0)
-    count(1)
     for du in (-1, 1, 2):
         links.arrive(sent["hu", -du if du != 2 else 2], rows_of(du, 0))
         to_v(du)
@@ -462,29 +485,28 @@
     from_v_far(1)
     add_group(core, turn(v, 1))
     add_group(core, turn(v, 2))
+    for c in (0, 1, -1, 2):
+        links.arrive(sent["across", c], column_half(turn(z_low, c), 1 - core))
+
+    def product(slab):
+        w = weights[slab].reshape(WIDTH, wide)
+        return jnp.dot(left_rows[slab], w, preferred_element_type=F32)
+
+    for n in range(SIDE):
+        own = hidden[core, y + core * (n - y), n + core * (y - n)]
+        left_rows[0, n * ROWS : (n + 1) * ROWS, :] = own
+    accumulated[...] = product(0)
     for dv in (-1, 1, 2):
         for du in order:
             links.arrive(crossed[du, dv], rows_of_peer(du, dv))
         add_group(1 - core, turn(u, dv))
-    for c in (0, 1, -1, 2):
-        links.arrive(sent["across", c], column_half(turn(z_low, c), 1 - core))
-
-    ring_rows = SIDE * ROWS
-    for n in range(SIDE):
-        own = hidden[core, y + core * (n - y), n + core * (y - n)]
-        left_rows[0, n * ROWS : (n + 1) * ROWS, :] = own
-        key = keys[n]
-        for r in range(RELATIONS):
-            low, high = float(r * BATCHES * ROWS), float((r + 1) * BATCHES * ROWS)
-            inside = jnp.where((key >= low) & (key < high), 1.0, 0.0)
-            number = jnp.maximum(jnp.sum(inside, axis=1, keepdims=True), 1.0)
-            some = slice(r * ring_rows + n * ROWS, r * ring_rows + (n + 1) * ROWS)
-            left_rows[r + 1, n * ROWS : (n + 1) * ROWS, :] = (summed[some, :] / number).astype(BF16)
-    total = jnp.zeros((ring_rows, wide), F32)
-    for slab in range(RELATIONS + 1):
-        w = weights[slab].reshape(WIDTH, wide)
-        total = total + jnp.dot(left_rows[slab], w, preferred_element_type=F32)
-    finished[...] = jnp.maximum(total, 0.0).astype(BF16).reshape(SIDE, ROWS, wide)
+    for r in range(RELATIONS):
+        some = slice(r * SIDE * ROWS, (r + 1) * SIDE * ROWS)
+        for c in range(WIDTH // LANES):
+            columns = slice(c * LANES, (c + 1) * LANES)
+            left_rows[r + 1, :, columns] = (summed[some, columns] * inverse[some, :]).astype(BF16)
+        accumulated[...] += product(r + 1)
+    finished[...] = jnp.maximum(accumulated[...], 0.0).astype(BF16).reshape(SIDE, ROWS, wide)
     for d in (1, -1, 2):
         sent["out", d] = links.send(finished.at[turn(x, d)], x_by[d], arrived.at[x])
     arrived[x] = finished[x]
@@ -512,12 +534,12 @@
             pltpu.SMEM(nbr.shape, jnp.int32),
             pltpu.VMEM(feats.shape, BF16),
             pltpu.VMEM(rel.shape, jnp.int32),
-            pltpu.VMEM((RELATIONS + 2, 64, WIDTH), BF16),
+            pltpu.VMEM((RELATIONS, 64, WIDTH), BF16),
             pltpu.VMEM((3, *ids.shape), jnp.int32),
             pltpu.VMEM((sources, LANES), F32),
             pltpu.VMEM((dest, 16), F32),
             pltpu.VMEM((2, FANOUT_ONE * 8, LANES), F32),
-            pltpu.VMEM((2 * ROWS, 3 * LANES), BF16),
+            pltpu.VMEM((2 * ROWS, 2 * LANES), BF16),
             pltpu.VMEM((LANES, 16), F32),
             pltpu.VMEM((SIDE, ROWS, LANES), F32),
             pltpu.VMEM((RELATIONS * SIDE * ROWS, BATCHES * ROWS), BF16),
@@ -528,12 +550,14 @@
             travelling,
             travelling,
             pltpu.VMEM((RELATIONS * SIDE * ROWS, WIDTH), F32),
+            pltpu.VMEM((RELATIONS * SIDE * ROWS, LANES), F32),
             pltpu.VMEM((RELATIONS + 1, SIDE * ROWS, WIDTH), BF16),
+            pltpu.VMEM((SIDE * ROWS, WIDTH // SIDE), F32),
             pltpu.VMEM((SIDE, ROWS, WIDTH // SIDE), BF16),
             pltpu.VMEM((SIDE, ROWS, WIDTH // SIDE), BF16),
             pltpu.SemaphoreType.DMA((COPIES,)),
             pltpu.SemaphoreType.DMA((COPIES,)),
-            pltpu.SemaphoreType.DMA((12,)),
+            pltpu.SemaphoreType.DMA((14,)),
         ],
         compiler_params=pltpu.CompilerParams(
             vmem_limit_bytes=62 << 20, collective_id=0, has_side_effects=True

time: 91.5 us -> 94 us (1.027)
  the two profiles are of different devices: /device:TPU:4 before, /device:TPU:8 now
where the time goes in v5:
time: 94 us; the launch traced here: 93.9 us
  Pallas kernels  92.3 us (98%)
  local copies, waits for them, and re-layouts  1.57 us (2%)
    pallas_call x1, Pallas kernels, two_layers(): pl.pallas_call(kernel, out_shape=jax.ShapeDtypeStruct((ROWS, WIDTH), BF16...  92.3 us

profile of v5, /device:TPU:8, one launch (start us, length us, event | category | flops | bytes accessed | tf_op | source)
XLA Modules:
  0.0 93.9 jit_solution(12003235319646161155)
XLA Ops:
  0.0 92.3 %two_layers.1 = bf16[64,1024]{1,0:T(8,128)(2,1)} custom-call(s32[15,8,128]{2,1,0:T(8,128)} %bitcast.17, bf16[48,8192]{1,0:T(8,128)(2,1)} %bitcast.15, s32[15,8,128]{2,1,0:T(8,128)} %bitcast.18, bf16[5,48,1024]{2,1,0:T(8,128)(2,1)} %w_one_hbm.1, s32[10,8,128]{2,1,0:T(8,128)} %bitcast.19, s32[10,8,128]{2,1,0:T(8,128)} %bitcast.20, s32[10,8,128]{2,1,0:T(8,128)} %bitcast.21, ...), custom_call_target="tpu_custom_call" | custom-call | flops 2400000000 | bytes 4000000 | tf_op jit(solution)/shard_map/two_layers/pallas_call | solution.py:528
  92.3 1.6 %copy.10 = bf16[1,64,1024]{2,1,0:T(8,128)(2,1)} copy(bf16[1,64,1024]{2,1,0:T(8,128)(2,1)} %bitcast.14) | data formatting | bytes 262144

commit v6 on v5

--- a/solution.py
+++ b/solution.py
@@ -54,11 +54,10 @@
 
 
 def build_table(feats, table, first, last):
-    gap = jnp.where(lax.broadcasted_iota(jnp.int32, (16, LANES), 0) == 15, 1.0, 0.0)
-
     def step(chunk, carry):
         at = pl.multiple_of(chunk * LANES, LANES)
         columns = feats[:, pl.ds(at, LANES)].astype(F32)
+        gap = jnp.zeros((LANES // 2 - columns.shape[0], LANES), F32)
         table[pl.ds(at, LANES), :] = jnp.concatenate([columns, gap, columns, gap], axis=0).T
         return carry
 
@@ -85,25 +84,20 @@
             source = nbr[k, row, column + i]
             picked[k * 8 + i : k * 8 + i + 1, :] = table[pl.ds(source, 1), :]
     zero = jnp.zeros(tile, F32)
-    low, high = zero, zero
+    low, high, low_count, high_count = zero, zero, zero, zero
     for k in range(FANOUT_ONE):
         rows = picked[k * 8 : (k + 1) * 8, :]
         own = jnp.broadcast_to(ids[:, k : k + 1], tile)
-        low = low + jnp.where(own == half, rows, 0.0)
-        high = high + jnp.where(own == half + 2.0, rows, 0.0)
-
-    def mean(total):
-        first = jnp.broadcast_to(total[:, 63:64], tile)
-        second = jnp.broadcast_to(total[:, 127:128], tile)
-        return total / jnp.maximum(jnp.where(half == 0.0, first, second), 1.0)
-
-    return mean(low), mean(high)
+        in_low, in_high = own == half, own == half + 2.0
+        low = low + jnp.where(in_low, rows, 0.0)
+        high = high + jnp.where(in_high, rows, 0.0)
+        low_count = low_count + jnp.where(in_low, 1.0, 0.0)
+        high_count = high_count + jnp.where(in_high, 1.0, 0.0)
+    return low / jnp.maximum(low_count, 1.0), high / jnp.maximum(high_count, 1.0)
 
 
 def gather_block(block, to, nbr, table, by_row, picked, slabs):
     row, start = block // 2, lax.rem(block, 2) * ROWS
-    lane = lax.broadcasted_iota(jnp.int32, (16, LANES), 1)
-    spare = lax.rem(lane, 64) >= 48
 
     def step(group, carry):
         at = pl.multiple_of(group * 16, 16)
@@ -112,18 +106,14 @@
             eight_means(base + n * 8, row, start + at + n * 8, nbr, table, by_row, picked.at[n])
             for n in range(2)
         ]
-        own = table[pl.ds(base, 16), :]
-        beside = (
-            jnp.where(lane < 64, pltpu.roll(own, 48, 1), pltpu.roll(own, 32, 1)),
-            pltpu.roll(own, 16, 1),
-        )
         for side in range(2):
             both = jnp.concatenate([pair[side] for pair in pairs], axis=0)
-            both = jnp.where(spare, beside[side], both)
             slabs[pl.ds(to + at, 16), side * LANES : (side + 1) * LANES] = both.astype(BF16)
         return carry
 
     lax.fori_loop(0, ROWS // 16, step, 0)
+    first = pl.multiple_of(block * ROWS, ROWS)
+    slabs[to : to + ROWS, 2 * LANES :] = table[pl.ds(first, ROWS), :].astype(BF16)
 
 
 def build_counts(keys, counts, first_row):
@@ -132,25 +122,16 @@
     def some_rows(n, carry):
         at = pl.multiple_of(n * 16, 16)
         key = keys[pl.ds(at, 16), :]
-        tiles = jnp.floor(key * (1.0 / LANES))
+        spread = [jnp.broadcast_to(key[:, k : k + 1], (16, LANES)) for k in range(FANOUT_TWO)]
         lane = lax.broadcasted_iota(jnp.int32, (16, LANES), 1).astype(F32)
-        tile_of, ones = [], []
-        for k in range(FANOUT_TWO):
-            column = jnp.broadcast_to(key[:, k : k + 1], (16, LANES))
-            tile = jnp.broadcast_to(tiles[:, k : k + 1], (16, LANES))
-            tile_of.append(tile.astype(BF16))
-            ones.append(jnp.where(column - tile * LANES == lane, 1.0, 0.0).astype(BF16))
-        zero = jnp.zeros((16, LANES), BF16)
         for r in range(RELATIONS):
             for c in range(span // LANES):
-                label = jnp.full((16, LANES), r * (span // LANES) + c, BF16)
-                parts = [
-                    jnp.where(tile_of[k] == label, ones[k], zero) for k in range(FANOUT_TWO)
-                ]
-                while len(parts) > 1:
-                    parts = [sum(parts[i : i + 2][1:], parts[i]) for i in range(0, len(parts), 2)]
+                label = lane + float(r * span + c * LANES)
+                total = jnp.zeros((16, LANES), F32)
+                for k in range(FANOUT_TWO):
+                    total = total + jnp.where(spread[k] == label, 1.0, 0.0)
                 rows = pl.ds(r * SIDE * ROWS + first_row + at, 16)
-                counts[rows, c * LANES : (c + 1) * LANES] = parts[0]
+                counts[rows, c * LANES : (c + 1) * LANES] = total.astype(BF16)
         return carry
 
     lax.fori_loop(0, ROWS // 16, some_rows, 0)
@@ -236,11 +217,8 @@
         (w_two.at[:, y, :, here], weights.at[:, z_high, z_low, y, :, lanes_of(core)]),
         (nbr_hbm, nbr),
         (rel_hbm, rel),
-        (w_one_hbm.at[pl.ds(1, RELATIONS)], w_one.at[:, pl.ds(0, 48)]),
-        *(
-            (w_one_hbm.at[pl.ds(0, 1), pl.ds(16 * n, 16)], w_one.at[pl.ds(n, 1), pl.ds(48, 16)])
-            for n in range(3)
-        ),
+        (w_one_hbm.at[pl.ds(1, RELATIONS)], w_one.at[pl.ds(0, RELATIONS), pl.ds(0, 48)]),
+        (w_one_hbm.at[pl.ds(0, 1)], w_one.at[pl.ds(RELATIONS, 1), pl.ds(0, 48)]),
         (owner_hbm, two.at[0]),
         (within_hbm, two.at[1]),
         (ids_hbm, two.at[2]),
@@ -347,7 +325,8 @@
     keys[x] = jnp.concatenate([columns_two[mine, :], none], axis=1)
     for d in (1, -1, 2):
         sent["keys", d] = links.send(keys.at[x], x_by[d])
-    w_one[3, 48:64, :] = jnp.zeros((16, WIDTH), BF16)
+    w_one[:, 48:64, :] = jnp.zeros((6, 16, WIDTH), BF16)
+    w_one[RELATIONS + 1, 0:48, :] = jnp.zeros((48, WIDTH), BF16)
 
     def count(d):
         n = turn(x, -d)
@@ -379,7 +358,7 @@
             columns = slice(h * quarter, (h + 1) * quarter)
             partial = jnp.dot(
                 slabs[0:rows, :],
-                w_one[:, :, columns].reshape(RELATIONS * 64, quarter),
+                w_one[:, :, columns].reshape(6 * 64, quarter),
                 preferred_element_type=F32,
             )
             if s == 0:
@@ -444,16 +423,24 @@
             links.arrive(sent["h", du, -2], half_of(rows_of(du, 2), 1))
         cross(du, 2)
 
-    def add_group(which, v_at, first=False):
-        group = which * SIDE + v_at
-        columns = pl.ds(pl.multiple_of(group * 2 * LANES, 2 * LANES), 2 * LANES)
+    def add_rows(dv, first=False):
+        for du in order:
+            links.arrive(crossed[du, dv], rows_of_peer(du, dv))
+        groups = ((core, turn(v, dv)), (1 - core, turn(u, dv)))
 
         def step(n, carry):
             at = pl.ds(pl.multiple_of(n * 256, 256), 256)
-            rows = hidden[which, v_at, :, :, at].reshape(SIDE * ROWS, 256)
+            rows = [hidden[which, group, :, :, at].reshape(SIDE * ROWS, 256) for which, group in groups]
             for r in range(RELATIONS):
                 some = slice(r * SIDE * ROWS, (r + 1) * SIDE * ROWS)
-                product = jnp.dot(counts[some, columns], rows, preferred_element_type=F32)
+                product = sum(
+                    jnp.dot(
+                        counts[some, pl.ds(pl.multiple_of((which * SIDE + group) * 256, 256), 256)],
+                        block,
+                        preferred_element_type=F32,
+                    )
+                    for (which, group), block in zip(groups, rows)
+                )
                 summed[some, at] = product if first else summed[some, at] + product
             return carry
 
@@ -464,27 +451,22 @@
     to_v(0)
     cross(0, 0)
 
+    count(-1)
+    count(2)
     for du in (-1, 1, 2):
         links.arrive(sent["hu", -du if du != 2 else 2], rows_of(du, 0))
         to_v(du)
         cross(du, 0)
-    count(-1)
     from_v(0)
-    count(2)
-    add_group(core, v, first=True)
-    for du in (-1, 1):
-        from_v(du)
-    for du in order:
-        links.arrive(crossed[du, 0], rows_of_peer(du, 0))
-    add_group(1 - core, u)
+    from_v(-1)
+    from_v(1)
+    add_rows(0, first=True)
     from_v_far(0)
     from_v(2)
-    add_group(core, turn(v, -1))
-    from_v_far(2)
-    from_v_far(-1)
-    from_v_far(1)
-    add_group(core, turn(v, 1))
-    add_group(core, turn(v, 2))
+    for du in (-1, 1, 2):
+        from_v_far(du)
+    add_rows(-1)
+    add_rows(1)
     for c in (0, 1, -1, 2):
         links.arrive(sent["across", c], column_half(turn(z_low, c), 1 - core))
 
@@ -496,10 +478,7 @@
         own = hidden[core, y + core * (n - y), n + core * (y - n)]
         left_rows[0, n * ROWS : (n + 1) * ROWS, :] = own
     accumulated[...] = product(0)
-    for dv in (-1, 1, 2):
-        for du in order:
-            links.arrive(crossed[du, dv], rows_of_peer(du, dv))
-        add_group(1 - core, turn(u, dv))
+    add_rows(2)
     for r in range(RELATIONS):
         some = slice(r * SIDE * ROWS, (r + 1) * SIDE * ROWS)
         for c in range(WIDTH // LANES):
@@ -534,12 +513,12 @@
             pltpu.SMEM(nbr.shape, jnp.int32),
             pltpu.VMEM(feats.shape, BF16),
             pltpu.VMEM(rel.shape, jnp.int32),
-            pltpu.VMEM((RELATIONS, 64, WIDTH), BF16),
+            pltpu.VMEM((RELATIONS + 2, 64, WIDTH), BF16),
             pltpu.VMEM((3, *ids.shape), jnp.int32),
             pltpu.VMEM((sources, LANES), F32),
             pltpu.VMEM((dest, 16), F32),
             pltpu.VMEM((2, FANOUT_ONE * 8, LANES), F32),
-            pltpu.VMEM((2 * ROWS, 2 * LANES), BF16),
+            pltpu.VMEM((2 * ROWS, 3 * LANES), BF16),
             pltpu.VMEM((LANES, 16), F32),
             pltpu.VMEM((SIDE, ROWS, LANES), F32),
             pltpu.VMEM((RELATIONS * SIDE * ROWS, BATCHES * ROWS), BF16),
@@ -557,7 +536,7 @@
             pltpu.VMEM((SIDE, ROWS, WIDTH // SIDE), BF16),
             pltpu.SemaphoreType.DMA((COPIES,)),
             pltpu.SemaphoreType.DMA((COPIES,)),
-            pltpu.SemaphoreType.DMA((14,)),
+            pltpu.SemaphoreType.DMA((12,)),
         ],
         compiler_params=pltpu.CompilerParams(
             vmem_limit_bytes=62 << 20, collective_id=0, has_side_effects=True

time: 94 us -> 96.5 us (1.027)
  the two profiles are of different devices: /device:TPU:8 before, /device:TPU:1 now
where the time goes in v6:
time: 96.5 us; the launch traced here: 96.3 us
  Pallas kernels  94.8 us (98%)
  local copies, waits for them, and re-layouts  1.57 us (2%)
    pallas_call x1, Pallas kernels, two_layers(): pl.pallas_call(kernel, out_shape=jax.ShapeDtypeStruct((ROWS, WIDTH), BF16...  94.8 us

profile of v6, /device:TPU:1, one launch (start us, length us, event | category | flops | bytes accessed | tf_op | source)
XLA Modules:
  0.0 96.3 jit_solution(17550325242975336996)
XLA Ops:
  0.0 94.8 %two_layers.1 = bf16[64,1024]{1,0:T(8,128)(2,1)} custom-call(s32[15,8,128]{2,1,0:T(8,128)} %bitcast.17, bf16[48,8192]{1,0:T(8,128)(2,1)} %bitcast.15, s32[15,8,128]{2,1,0:T(8,128)} %bitcast.18, bf16[5,48,1024]{2,1,0:T(8,128)(2,1)} %w_one_hbm.1, s32[10,8,128]{2,1,0:T(8,128)} %bitcast.19, s32[10,8,128]{2,1,0:T(8,128)} %bitcast.20, s32[10,8,128]{2,1,0:T(8,128)} %bitcast.21, ...), custom_call_target="tpu_custom_call" | custom-call | flops 2400000000 | bytes 4000000 | tf_op jit(solution)/shard_map/two_layers/pallas_call | solution.py:507
  94.8 1.6 %copy.10 = bf16[1,64,1024]{2,1,0:T(8,128)(2,1)} copy(bf16[1,64,1024]{2,1,0:T(8,128)(2,1)} %bitcast.14) | data formatting | bytes 262144

commit v7 on v6

--- a/solution.py
+++ b/solution.py
@@ -166,6 +166,7 @@
     from_left,
     from_right,
     summed,
+    near,
     inverse,
     left_rows,
     accumulated,
@@ -328,19 +329,6 @@
     w_one[:, 48:64, :] = jnp.zeros((6, 16, WIDTH), BF16)
     w_one[RELATIONS + 1, 0:48, :] = jnp.zeros((48, WIDTH), BF16)
 
-    def count(d):
-        n = turn(x, -d)
-        if d:
-            links.arrive(sent["keys", d], keys.at[n])
-        build_counts(keys.at[n], counts, n * ROWS)
-        key = keys[n]
-        for r in range(RELATIONS):
-            low, high = float(r * BATCHES * ROWS), float((r + 1) * BATCHES * ROWS)
-            inside = jnp.where((key >= low) & (key < high), 1.0, 0.0)
-            number = jnp.maximum(jnp.sum(inside, axis=1, keepdims=True), 1.0)
-            some = pl.ds(pl.multiple_of(r * SIDE * ROWS + n * ROWS, ROWS), ROWS)
-            inverse[some, :] = jnp.broadcast_to(1.0 / number, (ROWS, LANES))
-
     in_right, in_left = {}, {}
     steps = FEAT // 2
     quarter = WIDTH // 4
@@ -350,9 +338,6 @@
         if 0 < s < steps:
             gather_block(along(s - steps), ROWS, nbr, table, by_row, picked, slabs)
         serve(2 * s + 1)
-        if s == steps:
-            count(0)
-            count(1)
         rows = 2 * ROWS if 0 < s < steps else ROWS
         for h in range(4):
             columns = slice(h * quarter, (h + 1) * quarter)
@@ -373,7 +358,7 @@
                 links.arrive(in_right[s - 1, h], from_left.at[s - 1, h])
                 links.arrive(in_left[s - 1, h], from_right.at[s - 1, h])
                 total = partial + from_left[s - 1, h].astype(F32) + from_right[s - 1, h].astype(F32)
-                hidden[core, v, u, :, columns] = jnp.maximum(total, 0.0).astype(BF16)
+                hidden[0, 0, 0, :, columns] = jnp.maximum(total, 0.0).astype(BF16)
                 continue
             onward, back = partial[:ROWS], partial[ROWS:]
             if (s - 1, h) in in_right:
@@ -387,21 +372,24 @@
             send_left[s, h] = back.astype(BF16)
             in_left[s, h] = links.send(send_left.at[s, h], left, from_right.at[s, h])
 
-    def rows_of(du, dv):
-        return hidden.at[core, turn(v, dv), turn(u, du)]
+    def rows_of(du, dv, which=0):
+        return hidden.at[{0: 0, 1: 1, -1: 2, 2: 3}[dv], which, du % SIDE]
 
     def rows_of_peer(du, dv):
-        return hidden.at[1 - core, turn(u, dv), turn(v, du)]
+        return rows_of(du, dv, 1)
+
+    def opposite(d):
+        return d if d == 2 else -d
 
     order = (0, -1, 1, 2)
     crossed = {}
 
     def cross(du, dv):
-        crossed[du, dv] = links.send(rows_of(du, dv), peer)
+        crossed[du, dv] = links.send(rows_of(du, dv), peer, rows_of_peer(du, dv))
 
     def to_v(du):
         for d in (1, -1, 2) if du == 2 else (1, -1):
-            sent["h", du, d] = links.send(rows_of(du, 0), v_by[d])
+            sent["h", du, d] = links.send(rows_of(du, 0), v_by[d], rows_of(du, opposite(d)))
 
     def half_of(ref, which):
         return ref.at[pl.ds(which * (ROWS // 2), ROWS // 2)]
@@ -410,8 +398,9 @@
         for d in (1, -1):
             links.arrive(sent["h", du, d], rows_of(du, -d))
         if du != 2:
-            sent["h", du, 2] = links.send(half_of(rows_of(du, -1), 0), v_by[1])
-            sent["h", du, -2] = links.send(half_of(rows_of(du, 1), 1), v_by[-1])
+            far = rows_of(du, 2)
+            sent["h", du, 2] = links.send(half_of(rows_of(du, -1), 0), v_by[1], half_of(far, 0))
+            sent["h", du, -2] = links.send(half_of(rows_of(du, 1), 1), v_by[-1], half_of(far, 1))
         cross(du, -1)
         cross(du, 1)
 
@@ -423,50 +412,76 @@
             links.arrive(sent["h", du, -2], half_of(rows_of(du, 2), 1))
         cross(du, 2)
 
-    def add_rows(dv, first=False):
+    def add_rows(first, number):
+        depth = 2 * SIDE * ROWS
+        columns = slice(first * depth, (first + number) * depth)
+
+        def step(n, carry):
+            at = pl.ds(pl.multiple_of(n * 256, 256), 256)
+            rows = hidden[first : first + number, :, :, :, at].reshape(number * depth, 256)
+            for r in range(RELATIONS):
+                some = slice(r * SIDE * ROWS, (r + 1) * SIDE * ROWS)
+                value = jnp.dot(counts[some, columns], rows, preferred_element_type=F32)
+                if first:
+                    value = value + summed[some, at]
+                if first + number < SIDE:
+                    summed[some, at] = value
+                else:
+                    part = inverse[some, :]
+                    scaled = value * jnp.concatenate([part, part], axis=1)
+                    left_rows[r + 1, :, at] = scaled.astype(BF16)
+            return carry
+
+        lax.fori_loop(0, WIDTH // 256, step, 0)
+
+    def peer_rows(dv):
         for du in order:
             links.arrive(crossed[du, dv], rows_of_peer(du, dv))
-        groups = ((core, turn(v, dv)), (1 - core, turn(u, dv)))
-
-        def step(n, carry):
-            at = pl.ds(pl.multiple_of(n * 256, 256), 256)
-            rows = [hidden[which, group, :, :, at].reshape(SIDE * ROWS, 256) for which, group in groups]
-            for r in range(RELATIONS):
-                some = slice(r * SIDE * ROWS, (r + 1) * SIDE * ROWS)
-                product = sum(
-                    jnp.dot(
-                        counts[some, pl.ds(pl.multiple_of((which * SIDE + group) * 256, 256), 256)],
-                        block,
-                        preferred_element_type=F32,
-                    )
-                    for (which, group), block in zip(groups, rows)
-                )
-                summed[some, at] = product if first else summed[some, at] + product
-            return carry
-
-        lax.fori_loop(0, WIDTH // 256, step, 0)
 
     for d in (1, -1, 2):
-        sent["hu", d] = links.send(rows_of(0, 0), u_by[d])
+        sent["hu", d] = links.send(rows_of(0, 0), u_by[d], rows_of(opposite(d), 0))
     to_v(0)
     cross(0, 0)
 
-    count(-1)
-    count(2)
+    def count(d):
+        n = turn(x, -d)
+        if d:
+            links.arrive(sent["keys", d], keys.at[n])
+        key = keys[n].astype(jnp.int32)
+        holder = (key >> 6) & 31
+        same = (holder >> 4) == core
+        v_off = (((holder >> 2) & 3) - jnp.where(same, v, u)) & 3
+        u_off = ((holder & 3) - jnp.where(same, u, v)) & 3
+        place_of = (v_off ^ (v_off >> 1)) * (2 * SIDE) + jnp.where(same, 0, SIDE) + u_off
+        relation = key >> 11
+        near[...] = (relation * (BATCHES * ROWS) + place_of * ROWS + (key & 63)).astype(F32)
+        build_counts(near, counts, n * ROWS)
+        for r in range(RELATIONS):
+            inside = jnp.where(relation == r, 1.0, 0.0)
+            number = jnp.maximum(jnp.sum(inside, axis=1, keepdims=True), 1.0)
+            some = pl.ds(pl.multiple_of(r * SIDE * ROWS + n * ROWS, ROWS), ROWS)
+            inverse[some, :] = jnp.broadcast_to(1.0 / number, (ROWS, LANES))
+
+    count(0)
+    count(1)
     for du in (-1, 1, 2):
         links.arrive(sent["hu", -du if du != 2 else 2], rows_of(du, 0))
         to_v(du)
         cross(du, 0)
+    count(-1)
     from_v(0)
+    count(2)
     from_v(-1)
     from_v(1)
-    add_rows(0, first=True)
+    peer_rows(0)
+    add_rows(0, 1)
     from_v_far(0)
     from_v(2)
-    for du in (-1, 1, 2):
+    for du in (2, -1, 1):
         from_v_far(du)
-    add_rows(-1)
-    add_rows(1)
+    peer_rows(1)
+    peer_rows(-1)
+    add_rows(1, 2)
     for c in (0, 1, -1, 2):
         links.arrive(sent["across", c], column_half(turn(z_low, c), 1 - core))
 
@@ -475,15 +490,13 @@
         return jnp.dot(left_rows[slab], w, preferred_element_type=F32)
 
     for n in range(SIDE):
-        own = hidden[core, y + core * (n - y), n + core * (y - n)]
+        off = turn(n - x, 0)
+        own = hidden[core * (off + (off // 2) * (5 - 2 * off)), 0, (1 - core) * off]
         left_rows[0, n * ROWS : (n + 1) * ROWS, :] = own
     accumulated[...] = product(0)
-    add_rows(2)
+    peer_rows(2)
+    add_rows(3, 1)
     for r in range(RELATIONS):
-        some = slice(r * SIDE * ROWS, (r + 1) * SIDE * ROWS)
-        for c in range(WIDTH // LANES):
-            columns = slice(c * LANES, (c + 1) * LANES)
-            left_rows[r + 1, :, columns] = (summed[some, columns] * inverse[some, :]).astype(BF16)
         accumulated[...] += product(r + 1)
     finished[...] = jnp.maximum(accumulated[...], 0.0).astype(BF16).reshape(SIDE, ROWS, wide)
     for d in (1, -1, 2):
@@ -523,12 +536,13 @@
             pltpu.VMEM((SIDE, ROWS, LANES), F32),
             pltpu.VMEM((RELATIONS * SIDE * ROWS, BATCHES * ROWS), BF16),
             pltpu.VMEM((RELATIONS + 1, SIDE, SIDE, SIDE, ROWS // SIDE, WIDTH // SIDE), BF16),
-            pltpu.VMEM((2, SIDE, SIDE, ROWS, WIDTH), BF16),
+            pltpu.VMEM((SIDE, 2, SIDE, ROWS, WIDTH), BF16),
             travelling,
             travelling,
             travelling,
             travelling,
             pltpu.VMEM((RELATIONS * SIDE * ROWS, WIDTH), F32),
+            pltpu.VMEM((ROWS, LANES), F32),
             pltpu.VMEM((RELATIONS * SIDE * ROWS, LANES), F32),
             pltpu.VMEM((RELATIONS + 1, SIDE * ROWS, WIDTH), BF16),
             pltpu.VMEM((SIDE * ROWS, WIDTH // SIDE), F32),

time: 96.5 us -> 90.8 us (0.941)
  Pallas kernels: 94.8 us -> 89.1 us
    pallas_call x1, Pallas kernels: 94.8 us -> 89.1 us  [two_layers(): pl.pallas_call(kernel, out_shape=jax.ShapeDtypeStruct((ROWS, WIDTH), BF16...]
where the time goes in v7:
time: 90.8 us; the launch traced here: 90.7 us
  Pallas kernels  89.1 us (98%)
  local copies, waits for them, and re-layouts  1.57 us (2%)
    pallas_call x1, Pallas kernels, two_layers(): pl.pallas_call(kernel, out_shape=jax.ShapeDtypeStruct((ROWS, WIDTH), BF16...  89.1 us

profile of v7, /device:TPU:1, one launch (start us, length us, event | category | flops | bytes accessed | tf_op | source)
XLA Modules:
  0.0 90.7 jit_solution(3993862912478471359)
XLA Ops:
  0.0 89.1 %two_layers.1 = bf16[64,1024]{1,0:T(8,128)(2,1)} custom-call(s32[15,8,128]{2,1,0:T(8,128)} %bitcast.17, bf16[48,8192]{1,0:T(8,128)(2,1)} %bitcast.15, s32[15,8,128]{2,1,0:T(8,128)} %bitcast.18, bf16[5,48,1024]{2,1,0:T(8,128)(2,1)} %w_one_hbm.1, s32[10,8,128]{2,1,0:T(8,128)} %bitcast.19, s32[10,8,128]{2,1,0:T(8,128)} %bitcast.20, s32[10,8,128]{2,1,0:T(8,128)} %bitcast.21, ...), custom_call_target="tpu_custom_call" | custom-call | flops 2400000000 | bytes 4000000 | tf_op jit(solution)/shard_map/two_layers/pallas_call | solution.py:520
  89.1 1.6 %copy.10 = bf16[1,64,1024]{2,1,0:T(8,128)(2,1)} copy(bf16[1,64,1024]{2,1,0:T(8,128)(2,1)} %bitcast.14) | data formatting | bytes 262144

commit v8 on v7

--- a/solution.py
+++ b/solution.py
@@ -290,12 +290,9 @@
         6: [(y_far, 0)],
         7: [(y_step, 1), (y_step, -1)],
         8: [(y_step, 2)],
-        10: [(across_step, 0), (y_far, 1)],
+        10: [(y_far, 1)],
         11: [(y_far, -1)],
         12: [(y_far, 2)],
-        14: [(across_step, 1)],
-        15: [(across_step, -1)],
-        16: [(across_step, 2)],
     }
 
     def serve(slot):
@@ -462,6 +459,8 @@
             some = pl.ds(pl.multiple_of(r * SIDE * ROWS + n * ROWS, ROWS), ROWS)
             inverse[some, :] = jnp.broadcast_to(1.0 / number, (ROWS, LANES))
 
+    for c in (0, 1, -1, 2):
+        across_step(c)
     count(0)
     count(1)
     for du in (-1, 1, 2):

time: 90.8 us -> 90.8 us (level)
  no operation moved by 1% of the time
where the time goes in v8:
time: 90.8 us; the launch traced here: 90.6 us
  Pallas kernels  89 us (98%)
  local copies, waits for them, and re-layouts  1.57 us (2%)
    pallas_call x1, Pallas kernels, two_layers(): pl.pallas_call(kernel, out_shape=jax.ShapeDtypeStruct((ROWS, WIDTH), BF16...  89 us

profile of v8, /device:TPU:1, one launch (start us, length us, event | category | flops | bytes accessed | tf_op | source)
XLA Modules:
  0.0 90.6 jit_solution(4003984501038402613)
XLA Ops:
  0.0 89.0 %two_layers.1 = bf16[64,1024]{1,0:T(8,128)(2,1)} custom-call(s32[15,8,128]{2,1,0:T(8,128)} %bitcast.17, bf16[48,8192]{1,0:T(8,128)(2,1)} %bitcast.15, s32[15,8,128]{2,1,0:T(8,128)} %bitcast.18, bf16[5,48,1024]{2,1,0:T(8,128)(2,1)} %w_one_hbm.1, s32[10,8,128]{2,1,0:T(8,128)} %bitcast.19, s32[10,8,128]{2,1,0:T(8,128)} %bitcast.20, s32[10,8,128]{2,1,0:T(8,128)} %bitcast.21, ...), custom_call_target="tpu_custom_call" | custom-call | flops 2400000000 | bytes 4000000 | tf_op jit(solution)/shard_map/two_layers/pallas_call | solution.py:519
  89.1 1.6 %copy.10 = bf16[1,64,1024]{2,1,0:T(8,128)(2,1)} copy(bf16[1,64,1024]{2,1,0:T(8,128)(2,1)} %bitcast.14) | data formatting | bytes 262144
